TPU v7x, 256 devices: a whole 4x4x8 slice. The times are simulated.
256 devices in a mesh: row: 16 (over z_lo, x, core), col: 16 (over y, z_hi).
Axes of the slice: x: 4, y: 4, z: 8 (z_hi: 4, z_lo: 2; z = z_hi * 2 + z_lo), core: 2. Of those that a mesh axis runs over, the one named last changes fastest.
Arguments:
- pair_density: bfloat16 [4096, 8192], P('col', 'row'), may hold values from -6 to 6
- scale_exp: int32 [4096], replicated, may hold values from -1 to 1
- pair_weight: int32 [4096], replicated, may hold values from 1 to 4
- resident_ids: int32 [512], replicated, may hold values from 0 to 4095, as said below
- diagonal_shift: float32 [8192], replicated, may hold values from 2 to 4
- background: float32 [8192, 8192], P('row', 'col'), as said below
Outputs:
- dielectric: float32 [8192, 8192], P('row', 'col')
- kernel: float32 [4096, 512], P(('col', 'row'))
Inputs may be any that keep to these rules, and one draw needn't show every extreme that they name: `resident_ids`: 512 distinct pair indices. background is symmetric.
All inputs are finite; a program needn't handle non-finite values.
Results may differ from a plain program's by a relative error of at most 0.0003.
Values may be sent and summed in bfloat16 or wider, within the bound.
A program may use at most 64 MiB of HBM per device.

v0:
```python
import math

import jax
import jax.numpy as jnp
from jax import lax
from jax.sharding import PartitionSpec as P

NG = 8192
SWEEPS = 2


damping = 0.5


def from_root(block, axis, owner):
    block = jnp.where(lax.axis_index(axis) == owner, block, jnp.zeros_like(block))
    return lax.psum(block, axis)


def scale_factor(exponent):
    return jnp.where(exponent < 0, 0.5, jnp.where(exponent > 0, 2.0, 1.0)).astype(jnp.float32)


def pair_contract(left_block, right_block):
    return lax.dot_general(
        left_block, right_block, (((0,), (0,)), ((), ())), preferred_element_type=jnp.float32
    )


def shards(pair_density, scale_exp, pair_weight, resident_ids, diagonal_shift, background):
    row_count = lax.axis_size("row")
    col_count = lax.axis_size("col")
    row_index = lax.axis_index("row")
    col_index = lax.axis_index("col")
    pair_dev, row_width = pair_density.shape
    col_width = background.shape[1]
    pair_total = pair_dev * col_count
    norm_scale = 4 * pair_total
    factor = scale_factor(scale_exp)
    own_factor = lax.dynamic_slice_in_dim(factor, col_index * pair_dev, pair_dev)
    scaled = (pair_density.astype(jnp.float32) * own_factor[:, None]).astype(jnp.bfloat16)
    left_all = lax.all_gather(scaled, "col", axis=0, tiled=True)
    pair_rows_all = lax.all_gather(scaled, "row", axis=1, tiled=True)
    right_all = lax.all_to_all(pair_rows_all, "col", split_axis=1, concat_axis=0, tiled=True)
    contracted = pair_contract(left_all, right_all)
    response = contracted / norm_scale
    row_start = row_index * row_width
    col_start = col_index * col_width
    global_rows = row_start + lax.broadcasted_iota(jnp.int32, (row_width, col_width), 0)
    global_cols = col_start + lax.broadcasted_iota(jnp.int32, (row_width, col_width), 1)
    shift_rows = lax.dynamic_slice_in_dim(diagonal_shift, row_start, row_width)
    dielectric = (
        background + response + jnp.where(global_rows == global_cols, shift_rows[:, None], 0.0)
    )
    precond_rows = (
        shift_rows
        + jnp.einsum("pg,pg->g", left_all, left_all, preferred_element_type=jnp.float32)
        / norm_scale
    )
    picked = left_all[resident_ids].astype(jnp.float32) / factor[resident_ids][:, None]
    source_rows = picked.T
    col_ratio = col_count // row_count
    root_row = col_index // col_ratio
    source_cols, precond_cols = (
        from_root(source_rows, "row", root_row),
        from_root(precond_rows, "row", root_row),
    )
    screen_rows = source_rows / precond_rows[:, None]
    screen_cols = source_cols / precond_cols[:, None]
    for sweep_index in range(SWEEPS):
        last_sweep = sweep_index + 1 == SWEEPS
        row_image = lax.psum(
            jnp.dot(dielectric, screen_cols, precision=lax.Precision.HIGHEST), "col"
        )
        if not last_sweep:
            transposed = lax.dot_general(
                dielectric, screen_rows, (((0,), (0,)), ((), ())), precision=lax.Precision.HIGHEST
            )
            col_image = lax.psum(transposed, "row")
            screen_cols = screen_cols + damping * (source_cols - col_image) / precond_cols[:, None]
        screen_rows = screen_rows + damping * (source_rows - row_image) / precond_rows[:, None]
    partial_value = jnp.dot(
        pair_density.astype(jnp.float32), screen_rows, precision=lax.Precision.HIGHEST
    )
    summed = lax.psum_scatter(partial_value, "row", scatter_dimension=0, tiled=True)
    kernel_share = pair_dev // row_count
    weights = lax.dynamic_slice_in_dim(
        pair_weight, col_index * pair_dev + row_index * kernel_share, kernel_share
    ).astype(jnp.float32)
    kernel = weights[:, None] * summed / math.sqrt(NG)
    return (dielectric, kernel)


def solution(mesh):
    return jax.shard_map(
        shards,
        mesh=mesh,
        in_specs=(P("col", "row"), P(), P(), P(), P(), P("row", "col")),
        out_specs=(P("row", "col"), P(("col", "row"), None)),
        check_vma=False,
    )
```

profile of v0, /device:TPU:1, one launch (start us, length us, event | category | flops | bytes accessed | tf_op | source)
XLA Modules:
  0.0 607.4 jit_solution(10730562653668243322)
XLA Ops:
  7.2 0.0 all-gather.5.cloned.1.call-start
  7.2 0.7 select_select_fusion
  7.9 0.1 dynamic_slice.9
  8.0 1.8 multiply_convert_fusion
  9.8 0.0 all-gather.3.cloned.1.call-start
  9.8 0.7 all-gather.3.cloned.1.call-update
  10.6 44.0 %all-gather.5.cloned.1.call-done = bf16[256,8192]{1,0:T(8,128)(2,1)} async-done(((bf16[256,512]{1,0:T(8,128)(2,1)}), bf16[256,8192]{1,0:T(8,128)(2,1)}) %all-gather.5.cloned.1.call-update) | async-done | bytes 4194320 | tf_op jit(solution)/shard_map/all_gather | solution.py:43
  54.5 4.6 copy.26
  59.1 9.1 %all-to-all-start = ((bf16[256,16,512]{2,0,1:T(8,128)(2,1)}), bf16[256,16,512]{2,0,1:T(8,128)(2,1)}, u32[]{:S(2)}, u32[]{:S(2)}) async-start(bf16[256,16,512]{2,0,1:T(8,128)(2,1)} %bitcast.31), calls=%async_computation | async-start | bytes 8388608 | tf_op jit(solution)/shard_map/all_to_all | solution.py:44
  68.2 0.0 all-reduce.7.cloned.1.call-start
  68.3 3.1 gather_fusion.1
  71.5 132.9 %all-gather.3.cloned.1.call-done = bf16[4096,512]{1,0:T(8,128)(2,1)} async-done(((bf16[256,512]{1,0:T(8,128)(2,1)}), bf16[4096,512]{1,0:T(8,128)(2,1)}) %all-gather.3.cloned.1.call-update) | async-done | bytes 4194320 | tf_op jit(solution)/shard_map/all_gather | solution.py:42
  204.4 4.7 gather_fusion
  209.1 0.2 copy.14
  209.3 3.2 fusion
  212.5 0.8 broadcast_select_fusion
  213.3 1.2 fusion.16
  214.5 5.9 fusion.2
  220.4 3.2 fusion.17
  223.6 0.0 all-reduce.5.cloned.1.call-start
  223.7 27.1 %psum.36 = f32[512]{0:T(512)S(1)} all-reduce(f32[512]{0:T(512)S(1)} %get-tuple-element.12), channel_id=1, replica_groups=mesh['row'=16,'col'=16] {'row'}, use_global_device_ids=true, to_apply=%region_1.2 | all-reduce | flops 512 | bytes 4096 | tf_op jit(solution)/shard_map/psum | solution.py:17
  250.8 98.7 %all-reduce.7.cloned.1.call-done = (f32[512,512]{1,0:T(8,128)}, f32[512,512]{1,0:T(8,128)}) async-done(((f32[512,512]{1,0:T(8,128)}, f32[512,512]{1,0:T(8,128)}), (f32[512,512]{1,0:T(8,128)}, f32[512,512]{1,0:T(8,128)})) %all-reduce.7.cloned.1.call-update) | async-done | bytes 2097168 | tf_op jit(solution)/shard_map/psum | solution.py:17
  349.5 4.3 fusion.21
  353.9 3.1 fusion.7
  357.0 0.0 reduce-scatter.4.cloned.1.call-start
  357.0 172.1 %all-reduce.5.cloned.1.call-done = (f32[512,512]{1,0:T(8,128)}, f32[512,512]{1,0:T(8,128)}) async-done(((f32[512,512]{1,0:T(8,128)}, f32[512,512]{1,0:T(8,128)}), (f32[512,512]{1,0:T(8,128)}, f32[512,512]{1,0:T(8,128)})) %all-reduce.5.cloned.1.call-update) | async-done | bytes 2097168 | tf_op jit(solution)/shard_map/psum | solution.py:72
  529.1 2.9 convolution_bitcast_fusion
  532.0 1.0 copy.22
  533.0 0.8 dynamic-slice_convert_fusion
  533.8 65.5 %reduce-scatter.4.cloned.1.call-done = f32[16,512]{1,0:T(8,128)} async-done(((f32[256,512]{1,0:T(8,128)}), f32[16,512]{1,0:T(8,128)}) %reduce-scatter.4.cloned.1.call-update) | async-done | bytes 32784
  599.2 0.9 copy.23
  600.2 0.7 copy.15
  (21 shorter events, 0.1 us)
Async XLA Ops:
  7.2 47.4 %all-gather.5.cloned.1.call-start = ((), (), s32[]{:S(2)}) async-start(), calls=%async_computation.3 | async-start | bytes 4456448 | tf_op jit(solution)/shard_map/all_gather | solution.py:43
  9.8 194.6 %all-gather.3.cloned.1.call-start = ((), (), s32[]{:S(2)}) async-start(), calls=%async_computation.2 | async-start | bytes 4456448 | tf_op jit(solution)/shard_map/all_gather | solution.py:42
  59.1 9.1 %copy-start.1 = (s32[512]{0:T(512)S(1)}, s32[512]{0:T(512)}, u32[]{:S(2)}) copy-start(s32[512]{0:T(512)} %param.9) | copy-start | bytes 6148
  59.1 155.4 %all-to-all-start = ((bf16[256,16,512]{2,0,1:T(8,128)(2,1)}), bf16[256,16,512]{2,0,1:T(8,128)(2,1)}, u32[]{:S(2)}, u32[]{:S(2)}) async-start(bf16[256,16,512]{2,0,1:T(8,128)(2,1)} %bitcast.31), calls=%async_computation | async-start | bytes 8388608 | tf_op jit(solution)/shard_map/all_to_all | solution.py:44
  68.2 281.3 %all-reduce.7.cloned.1.call-start = ((), (), s32[]{:S(2)}) async-start(), calls=%async_computation.6 | async-start | bytes 4194304 | tf_op jit(solution)/shard_map/psum | solution.py:17
  209.1 5.4 copy-start.2
  220.4 133.4 %copy-start.5 = (f32[512,512]{1,0:T(8,128)}, f32[512,512]{1,0:T(8,128)S(1)}, u32[]{:S(2)}) copy-start(f32[512,512]{1,0:T(8,128)S(1)} %fusion.2) | copy-start | bytes 3145732
  223.6 305.5 %all-reduce.5.cloned.1.call-start = ((), (), s32[]{:S(2)}) async-start(), calls=%async_computation.5 | async-start | bytes 4194304 | tf_op jit(solution)/shard_map/psum | solution.py:72
  349.5 4.3 copy-start.3
  349.5 4.3 copy-start.4
  353.8 175.3 %copy-start = (bf16[256,512]{1,0:T(8,128)(2,1)S(1)}, bf16[256,512]{1,0:T(8,128)(2,1)}, u32[]{:S(2)}) copy-start(bf16[256,512]{1,0:T(8,128)(2,1)} %param.6) | copy-start | bytes 786436
  357.0 242.3 %reduce-scatter.4.cloned.1.call-start = ((), (), s32[]{:S(2)}) async-start(), calls=%async_computation.4 | async-start | bytes 557056
Sparse Core Ops, SparseCore 0:
  10.4 44.1 all-gather.4
  57.5 146.7 all-gather.2
  223.7 125.7 all-reduce.6
  357.1 171.9 all-reduce.4
  533.1 66.0 reduce-scatter.3
where the time goes:
time: 610 us; the launch traced here: 607 us
  waiting for transfers between devices  514 us (84%)
  blocking collectives  27.1 us (4%)
  matrix products  19.3 us (3%)
  local copies, waits for them, and re-layouts  15.4 us (3%)
  between operations  13.9 us (2%)
  starting transfers between devices  9.27 us (2%)
  other arithmetic  8.49 us (1%)
    psum x1, waiting for transfers between devices, shards(): lax.psum(jnp.dot(dielectric, screen_cols, precision=lax.Precision.HIGHEST...  172 us
    all_gather x1, waiting for transfers between devices, shards(): left_all = lax.all_gather(scaled, 'col', axis=0, tiled=True)  133 us
    psum x1, waiting for transfers between devices, from_root(): return lax.psum(block, axis)  98.7 us
    unnamed x6, waiting for transfers between devices  66.2 us
    all_gather x1, waiting for transfers between devices, shards(): pair_rows_all = lax.all_gather(scaled, 'row', axis=1, tiled=True)  44 us
    psum x1, blocking collectives, from_root(): return lax.psum(block, axis)  27.1 us
  transfers between devices with their start and end apart: 6, of which 5 were waited for; matrix products, arithmetic and copies ran while one was open for 3% of the time, Pallas kernels for 0%

commit v1 on v0

v1 whole, which is shorter than its diff:
```python
import math

import jax
import jax.numpy as jnp
from jax import lax
from jax.experimental import pallas as pl
from jax.experimental.pallas import tpu as pltpu
from jax.sharding import PartitionSpec as P

NG = 8192
NRES = 512
MESH = pl.DeviceIdType.MESH
BF = jnp.bfloat16
F32 = jnp.float32


class Place:
    def __init__(self):
        self.r = lax.axis_index("row")
        self.c = lax.axis_index("col")
        self.zl = self.r // 8
        self.x = (self.r // 2) % 4
        self.k = self.r % 2
        self.y = self.c // 4
        self.h = self.c % 4

    def row(self, zl=0, x=0, k=0):
        return ((self.zl + zl) % 2) * 8 + ((self.x + x) % 4) * 2 + (self.k + k) % 2

    def col(self, y=0, h=0):
        return ((self.y + y) % 4) * 4 + (self.h + h) % 4


def remote(src, dst, send, recv, row, col):
    return pltpu.make_async_remote_copy(
        src_ref=src, dst_ref=dst, send_sem=send, recv_sem=recv,
        device_id=(row, col), device_id_type=MESH,
    )


def greet(partners, me=None):
    barrier = pltpu.get_barrier_semaphore()
    for row, col in partners:
        pl.semaphore_signal(barrier, inc=1, device_id=(row, col), device_id_type=MESH)
    if me is not None:
        @pl.when(me.r != me.c)
        def _():
            pl.semaphore_signal(barrier, inc=1, device_id=(me.c, me.r), device_id_type=MESH)
    count = len(partners)
    if me is not None:
        count = count + jnp.where(me.r != me.c, 1, 0)
    pl.semaphore_wait(barrier, count)


class Ring:
    def __init__(self, send, recv, base, slots, step):
        self.send, self.recv, self.base, self.slots, self.step = send, recv, base, slots, step
        self.sent = []

    def copy(self, n, ref, d):
        one = remote(ref, ref, self.send.at[self.base + n], self.recv.at[self.base + n], *self.step(d))
        return one

    def start(self):
        for n, d in ((0, 1), (1, -1)):
            one = self.copy(n, self.slots(0), d)
            one.start()
            self.sent.append(one)

    def halves(self, d, n):
        rows = self.slots(0).shape[0] // 2
        return self.slots(d).at[pl.ds(n * rows, rows)]

    def forward(self):
        for n, d in ((0, 1), (1, -1)):
            self.copy(n, self.slots(-d), d).wait_recv()
            one = self.copy(2 + n, self.halves(-d, n), d)
            one.start()
            self.sent.append(one)

    def last(self):
        for n, d in ((0, 1), (1, -1)):
            self.copy(2 + n, self.halves(-2 * d, n), d).wait_recv()

    def drain(self):
        for one in self.sent:
            one.wait_send()


def gather_kernel(a_ref, al, ar, zs, zr, ys, yr, xs, xr, ls, lr, ks, kr, ts, tr, own_sem):
    me = Place()
    greet(
        [(me.r, me.col(h=1)), (me.r, me.col(h=-1)), (me.r, me.col(y=1)), (me.r, me.col(y=-1)),
         (me.row(x=1), me.c), (me.row(x=-1), me.c), (me.row(zl=1), me.c), (me.row(k=1), me.c)],
        me,
    )
    own = pltpu.make_async_copy(a_ref, al.at[me.c], own_sem.at[0])
    own.start()
    diag = pltpu.make_async_copy(a_ref, ar.at[me.r], own_sem.at[1])
    turn = remote(a_ref, ar.at[me.c], ts, tr, me.c, me.r)
    turned = remote(ar.at[me.r], ar.at[me.r], ts, tr, me.c, me.r)

    @pl.when(me.r == me.c)
    def _():
        diag.start()

    own.wait()
    z = Ring(zs, zr, 0, lambda d: al.at[me.col(h=d)], lambda d: (me.r, me.col(h=d)))
    z.start()
    offsets = (0, -1, 1, 2)
    yy = [
        Ring(ys, yr, 4 * n, lambda d, o=o: al.at[me.col(y=d, h=o)], lambda d: (me.r, me.col(y=d)))
        for n, o in enumerate(offsets)
    ]

    @pl.when(me.r != me.c)
    def _():
        turn.start()

    yy[0].start()

    @pl.when(me.r != me.c)
    def _():
        turned.wait_recv()

    @pl.when(me.r == me.c)
    def _():
        diag.wait()

    xx = [
        Ring(xs, xr, 4 * n, lambda d, n=n: ar.at[me.row(zl=n, x=d)], lambda d: (me.row(x=d), me.c))
        for n in range(2)
    ]
    low = remote(ar.at[me.r], ar.at[me.r], ls, lr, me.row(zl=1), me.c)
    low_in = remote(ar.at[me.row(zl=1)], ar.at[me.row(zl=1)], ls, lr, me.row(zl=1), me.c)
    low.start()
    xx[0].start()
    cores = []

    def hand(n, d):
        ref = ar.at[me.row(zl=n, x=d)]
        one = remote(ref, ref, ks.at[len(cores)], kr.at[len(cores)], me.row(k=1), me.c)
        one.start()
        there = ar.at[me.row(zl=n, x=d, k=1)]
        cores.append((one, remote(there, there, ks.at[len(cores)], kr.at[len(cores)], me.row(k=1), me.c)))

    hand(0, 0)
    yy[0].forward()
    z.forward()
    yy[1].start()
    yy[2].start()
    low_in.wait_recv()
    xx[1].start()
    hand(1, 0)
    xx[0].forward()
    hand(0, 1)
    hand(0, -1)
    z.last()
    yy[3].start()
    yy[1].forward()
    yy[2].forward()
    xx[1].forward()
    hand(1, 1)
    hand(1, -1)
    xx[0].last()
    hand(0, 2)
    yy[3].forward()
    xx[1].last()
    hand(1, 2)
    for one in yy:
        one.last()
    for one, arrived in cores:
        arrived.wait_recv()
    for one in [z, *yy, *xx]:
        one.drain()
    for one, arrived in cores:
        one.wait_send()
    low.wait_send()

    @pl.when(me.r != me.c)
    def _():
        turn.wait_send()


def gather(scaled):
    depth, width = scaled.shape
    shape = jax.ShapeDtypeStruct((16, depth, width), scaled.dtype)
    dma = pltpu.SemaphoreType.DMA
    left, right = pl.pallas_call(
        gather_kernel,
        out_shape=(shape, shape),
        in_specs=[pl.BlockSpec(memory_space=pl.ANY)],
        out_specs=(pl.BlockSpec(memory_space=pl.ANY),) * 2,
        scratch_shapes=[
            dma((4,)), dma((4,)), dma((16,)), dma((16,)), dma((8,)), dma((8,)),
            dma, dma, dma((8,)), dma((8,)), dma, dma, dma((2,)),
        ],
        compiler_params=pltpu.CompilerParams(collective_id=0, has_side_effects=True),
        cost_estimate=pl.CostEstimate(flops=0, bytes_accessed=16 << 20, transcendentals=0),
        name="gather_panels",
    )(scaled)
    return left, right


def split(value):
    high = value.astype(BF)
    return high, (value - high.astype(F32)).astype(BF)


def nn(a, b):
    return lax.dot_general(a, b, (((1,), (0,)), ((), ())), preferred_element_type=F32)


def nt(a, b):
    return lax.dot_general(a, b, (((1,), (1,)), ((), ())), preferred_element_type=F32)


def rows(start, size):
    return pl.ds(pl.multiple_of(start * size, size), size)


PEERS = [(a, b) for a in range(2) for b in range(4) if (a, b) != (0, 0)]


def sweep_kernel(
    dp, src_r, src_c, pr, pc, al, weight, out,
    dh, dl, sh, sl, u1, xbuf, wbuf, rbuf, s1, u2, ybuf, tbuf, hbuf, kp, kx, ko, kbuf, kt, fin,
    cs, cr, rs, rr, gs, gr, fs, fr, ys, yr, hs, hr, k1s, k1r, k2s, k2r, as_, ar_,
):
    me = Place()
    greet(
        [(me.row(k=1), me.c)]
        + [(me.row(zl=a, x=b), me.c) for a, b in PEERS]
        + [(me.r, (me.c + d) % 16) for d in range(1, 16)]
    )
    j = me.zl * 4 + me.x
    sent = []

    def go(one):
        one.start()
        sent.append(one)

    def peer_j(a, b):
        return ((me.zl + a) % 2) * 4 + (me.x + b) % 4

    high, low = split(dp[...])
    dh[...] = high
    dl[...] = low
    high, low = split(src_r[...].astype(F32) / pr[...])
    sh[...] = high
    sl[...] = low

    def first(k):
        at = rows(k, 256)
        u1[at, :] = nn(sh[at, :], dh[...]) + nn(sh[at, :], dl[...]) + nn(sl[at, :], dh[...])

    other = 1 - me.k
    first(other)
    swap = remote(u1.at[rows(other, 256)], xbuf, cs.at[0], cr.at[0], me.row(k=1), me.c)
    go(swap)
    first(me.k)
    swap.wait_recv()
    wbuf[...] = (u1[rows(me.k, 256), :] + xbuf[...]).reshape(8, 32, 512)
    ones = []
    for n, (a, b) in enumerate(PEERS):
        one = remote(wbuf.at[peer_j(a, b)], rbuf.at[n], rs.at[n], rr.at[n], me.row(zl=a, x=b), me.c)
        go(one)
        ones.append(one)
    total = wbuf[j]
    for n, one in enumerate(ones):
        one.wait_recv()
        total = total + rbuf[n]
    q = me.k * 8 + j
    high, low = split((0.5 * src_c[rows(q, 32), :].astype(F32) + total) / pc[...])
    s1[q, 0] = high
    s1[q, 1] = low
    for n, (a, b) in enumerate(PEERS):
        go(remote(s1.at[q], s1.at[q], gs.at[n], gr.at[n], me.row(zl=a, x=b), me.c))
    hands = []

    def hand(n, jj):
        ref = s1.at[me.k * 8 + jj]
        go(remote(ref, ref, fs.at[n], fr.at[n], me.row(k=1), me.c))
        there = s1.at[other * 8 + jj]
        hands.append(remote(there, there, fs.at[n], fr.at[n], me.row(k=1), me.c))

    hand(7, j)
    for n, (a, b) in enumerate(PEERS):
        jj = peer_j(-a, -b)
        ref = s1.at[me.k * 8 + jj]
        remote(ref, ref, gs.at[n], gr.at[n], me.row(zl=a, x=b), me.c).wait_recv()
        hand(n, jj)

    def second(k):
        sl1 = s1[pl.ds(k * 8, 8), 1].reshape(256, 512)
        sh1 = s1[pl.ds(k * 8, 8), 0].reshape(256, 512)
        u2[rows(k, 256), :] = nt(sh1, dh[...]) + nt(sh1, dl[...]) + nt(sl1, dh[...])

    second(me.k)
    for one in hands:
        one.wait_recv()
    second(other)
    ones = []
    for d in range(1, 4):
        one = remote(
            u2.at[rows((me.y + d) % 4, 128)], ybuf.at[d - 1], ys.at[d - 1], yr.at[d - 1],
            me.r, me.col(y=d),
        )
        go(one)
        ones.append(one)
    total = u2[rows(me.y, 128), :]
    for d, one in enumerate(ones):
        one.wait_recv()
        total = total + ybuf[d]
    tbuf[...] = total.reshape(4, 32, 512)
    ones = []
    for d in range(1, 4):
        one = remote(
            tbuf.at[(me.h + d) % 4], hbuf.at[d - 1], hs.at[d - 1], hr.at[d - 1], me.r, me.col(h=d)
        )
        go(one)
        ones.append(one)
    total = tbuf[me.h]
    for d, one in enumerate(ones):
        one.wait_recv()
        total = total + hbuf[d]
    high, low = split((0.5 * src_r[rows(me.c, 32), :].astype(F32) + total) / pr[...])
    both = jnp.concatenate([high, low], axis=0)

    def third(ref, k):
        for jj in range(8):
            part = nt(both, al[:, jj * 2 + k].reshape(256, 512))
            ref[jj] = part[:32] + part[32:]

    third(kp, other)
    swap = remote(kp, kx, cs.at[1], cr.at[1], me.row(k=1), me.c)
    go(swap)
    third(ko, me.k)
    swap.wait_recv()
    ko[...] += kx[...]
    ones = []
    for n, (a, b) in enumerate(PEERS):
        one = remote(ko.at[peer_j(a, b)], kbuf.at[n], k1s.at[n], k1r.at[n], me.row(zl=a, x=b), me.c)
        go(one)
        ones.append(one)
    total = ko[j]
    for n, one in enumerate(ones):
        one.wait_recv()
        total = total + kbuf[n]
    turned = jnp.concatenate([total.T, jnp.zeros((256, 96), F32)], axis=1)
    kt[...] = turned.reshape(16, 16, 128)
    fin[me.c] = kt[me.c]
    for d in range(1, 16):
        to = (me.c + d) % 16
        go(remote(kt.at[to], fin.at[me.c], as_.at[d], ar_.at[d], me.r, to))
    for d in range(1, 16):
        ref = fin.at[(me.c - d) % 16]
        remote(ref, ref, as_.at[d], ar_.at[d], me.r, (me.c + d) % 16).wait_recv()
    out[...] = jnp.concatenate([fin[n][:, :32] for n in range(16)], axis=1) * weight[...]
    for one in sent:
        one.wait_send()


def sweep(dp, src_r, src_c, pr, pc, al, weight):
    dma = pltpu.SemaphoreType.DMA
    vmem = pltpu.VMEM
    sems = []
    for n in (2, 7, 7, 8, 3, 3, 7, 7, 16):
        sems += [dma((n,)), dma((n,))]
    return pl.pallas_call(
        sweep_kernel,
        out_shape=jax.ShapeDtypeStruct((16, NRES), F32),
        in_specs=[pl.BlockSpec(memory_space=pltpu.VMEM)] * 7,
        out_specs=pl.BlockSpec(memory_space=pltpu.VMEM),
        scratch_shapes=[
            vmem((512, 512), BF), vmem((512, 512), BF), vmem((512, 512), BF), vmem((512, 512), BF),
            vmem((512, 512), F32), vmem((256, 512), F32), vmem((8, 32, 512), F32), vmem((7, 32, 512), F32),
            vmem((16, 2, 32, 512), BF), vmem((512, 512), F32), vmem((3, 128, 512), F32),
            vmem((4, 32, 512), F32), vmem((3, 32, 512), F32),
            vmem((8, 32, 256), F32), vmem((8, 32, 256), F32), vmem((8, 32, 256), F32),
            vmem((7, 32, 256), F32), vmem((16, 16, 128), F32), vmem((16, 16, 128), F32),
        ] + sems,
        compiler_params=pltpu.CompilerParams(
            collective_id=1, has_side_effects=True, vmem_limit_bytes=48 << 20
        ),
        name="sweeps",
    )(dp, src_r, src_c, pr, pc, al, weight)


def scale_factor(exponent):
    return jnp.where(exponent < 0, 0.5, jnp.where(exponent > 0, 2.0, 1.0)).astype(F32)


def shards(pair_density, scale_exp, pair_weight, resident_ids, diagonal_shift, background):
    row_index = lax.axis_index("row")
    col_index = lax.axis_index("col")
    pair_dev, row_width = pair_density.shape
    col_width = background.shape[1]
    norm_scale = 4 * pair_dev * 16
    factor = scale_factor(scale_exp)
    own_factor = lax.dynamic_slice_in_dim(factor, col_index * pair_dev, pair_dev)
    scaled = (pair_density.astype(F32) * own_factor[:, None]).astype(BF)
    left, right = gather(scaled)
    left_all = left.reshape(-1, row_width)
    right_all = right.reshape(-1, col_width)
    response = lax.dot_general(
        left_all, right_all, (((0,), (0,)), ((), ())), preferred_element_type=F32
    ) / norm_scale
    row_start = row_index * row_width
    col_start = col_index * col_width
    global_rows = row_start + lax.broadcasted_iota(jnp.int32, (row_width, col_width), 0)
    global_cols = col_start + lax.broadcasted_iota(jnp.int32, (row_width, col_width), 1)
    shift_rows = lax.dynamic_slice_in_dim(diagonal_shift, row_start, row_width)
    shift_cols = lax.dynamic_slice_in_dim(diagonal_shift, col_start, col_width)
    on_diagonal = global_rows == global_cols
    dielectric = background + response + jnp.where(on_diagonal, shift_rows[:, None], 0.0)

    def precond_of(panel, shift):
        return shift + jnp.einsum("pg,pg->g", panel, panel, preferred_element_type=F32) / norm_scale

    precond_rows = precond_of(left_all, shift_rows)
    precond_cols = precond_of(right_all, shift_cols)
    inverse = (1.0 / factor[resident_ids])[:, None]
    source_rows = (left_all[resident_ids].astype(F32) * inverse).astype(BF)
    source_cols = (right_all[resident_ids].astype(F32) * inverse).astype(BF)
    step = jnp.where(on_diagonal, precond_rows[:, None], 0.0) - 0.5 * dielectric
    start = col_index * pair_dev + row_index * 16
    weights = lax.dynamic_slice_in_dim(pair_weight, start, 16).astype(F32)
    weights = weights / lax.dynamic_slice_in_dim(factor, start, 16) / math.sqrt(NG)
    kernel = sweep(
        step, source_rows, source_cols, precond_rows[None], precond_cols[None],
        left.reshape(16, 16, 16, row_width), weights[:, None],
    )
    return (dielectric, kernel)


def solution(mesh):
    return jax.shard_map(
        shards,
        mesh=mesh,
        in_specs=(P("col", "row"), P(), P(), P(), P(), P("row", "col")),
        out_specs=(P("row", "col"), P(("col", "row"), None)),
        check_vma=False,
    )
```

time: 610 us -> 172 us (0.28)
  waiting for transfers between devices: 514 us -> 0 us
  Pallas kernels: 0 us -> 141 us
  blocking collectives: 27.1 us -> 0 us
  between operations: 13.9 us -> 0.72 us
  matrix products: 19.3 us -> 6.94 us
  starting transfers between devices: 9.27 us -> 0 us
    psum x2 -> x0, waiting for transfers between devices: 271 us -> none  [the longest x1 172 us: shards(): lax.psum(jnp.dot(dielectric, screen_cols, precision=lax.Precision.HIGHEST...]
    all_gather x2 -> x0, waiting for transfers between devices: 177 us -> none  [the longest x1 133 us: shards(): left_all = lax.all_gather(scaled, 'col', axis=0, tiled=True)]
    pallas_call x0 -> x2, Pallas kernels: none -> 141 us  [the longest x1 73.2 us: gather(): pl.pallas_call(gather_kernel, out_shape=(shape, shape), in_specs=[pl.Bloc...]
    unnamed x6 -> x0, waiting for transfers between devices: 66.2 us -> none
    psum x1 -> x0, blocking collectives: 27.1 us -> none  [from_root(): return lax.psum(block, axis)]
    dot_general x5 -> x1, matrix products: 19.3 us -> 6.94 us  [shards(): lax.dot_general(left_all, right_all, (((0,), (0,)), ((), ())), preferred_...]
    all_to_all x1 -> x0, starting transfers between devices: 9.07 us -> none  [shards(): lax.all_to_all(pair_rows_all, 'col', split_axis=1, concat_axis=0, tiled=T...]
  transfers between devices with their start and end apart: 6 -> 0, of which waited for: 5 -> 0; matrix products, arithmetic and copies ran while one was open for 3% -> 0% of each run, Pallas kernels for 0% -> 0%
where the time goes in v1:
time: 172 us
  Pallas kernels  141 us (82%)
  local copies, waits for them, and re-layouts  13.4 us (8%)
  other arithmetic  9.59 us (6%)
  matrix products  6.94 us (4%)
    pallas_call x1, Pallas kernels, gather(): pl.pallas_call(gather_kernel, out_shape=(shape, shape), in_specs=[pl.Bloc...  73.2 us
    pallas_call x1, Pallas kernels, sweep(): pl.pallas_call(sweep_kernel, out_shape=jax.ShapeDtypeStruct((16, NRES), F...  68.1 us
    dot_general x1, matrix products, shards(): lax.dot_general(left_all, right_all, (((0,), (0,)), ((), ())), preferred_...  6.94 us
    dot_general x1, other arithmetic, precond_of(): jnp.einsum('pg,pg->g', panel, panel, preferred_element_type=F32)  5.24 us
    gather x1, local copies, waits for them, and re-layouts, shards(): source_rows = (left_all[resident_ids].astype(F32) * inverse).astype(BF)  4.71 us
    gather x1, local copies, waits for them, and re-layouts, shards(): source_cols = (right_all[resident_ids].astype(F32) * inverse).astype(BF)  4.71 us

profile of v1, /device:TPU:1, one launch (start us, length us, event | category | flops | bytes accessed | tf_op | source)
XLA Modules:
  0.0 171.9 jit_solution(17938905347006410401)
XLA Ops:
  0.6 0.7 select_select_fusion
  1.4 0.1 dynamic_slice.15
  1.4 1.8 %multiply_convert_fusion.2.a_ref = bf16[256,512]{1,0:T(8,128)(2,1)} fusion(bf16[256,512]{1,0:T(8,128)(2,1)} %param.6, f32[256]{0:T(256)S(1)} %dynamic_slice.15), kind=kLoop, calls=%fused_computation.16 | loop fusion | flops 393216 | bytes 525312 | tf_op jit(solution)/shard_map/convert_element_type | solution.py:402
  3.2 73.2 %gather_panels.1 = (bf16[16,256,512]{2,1,0:T(8,128)(2,1)}, bf16[16,256,512]{2,1,0:T(8,128)(2,1)}) custom-call(bf16[256,512]{1,0:T(8,128)(2,1)} %multiply_convert_fusion.2.a_ref), custom_call_target="tpu_custom_call" | custom-call | bytes 16777216 | tf_op jit(solution)/shard_map/gather_panels/pallas_call | solution.py:189
  76.4 0.0 copy-start.1
  76.4 5.2 %fusion = (f32[512]{0:T(512)S(1)}, f32[512]{0:T(512)S(1)}) fusion(bf16[16,256,512]{2,1,0:T(8,128)(2,1)} %get-tuple-element.5, bf16[16,256,512]{2,1,0:T(8,128)(2,1)} %get-tuple-element.4), kind=kLoop, calls=%fused_computation.4 | loop fusion | flops 12581888 | bytes 8392704 | tf_op jit(solution)/shard_map/pg,pg->g/dot_general | solution.py:419
  81.6 0.8 multiply_add_fusion.1
  82.5 0.0 copy-done.1
  82.5 0.0 copy-start
  82.5 6.9 %fusion.5 = (f32[512,512]{1,0:T(8,128)S(1)}, f32[512,512]{1,0:T(8,128)}) fusion(f32[512]{0:T(512)S(1)} %get-tuple-element.6, s32[512]{0:T(512)S(1)} %get-tuple-element.15, s32[512]{0:T(512)S(1)} %get-tuple-element.16, f32[512]{0:T(512)S(1)} %get-tuple-element.7, f32[512,512]{1,0:T(8,128)S(1)} %copy-done.1, bf16[16,256,512]{2,1,0:T(8,128)(2,1)} %get-tuple-element.4, ...), kind=kOutput, calls=%fused_computation.13 | convolution fusion | flops 2149580800 | bytes 11542528 | tf_op jit(solution)/shard_map/dot_general | solution.py:406
  89.4 0.0 copy-done
  89.5 4.7 %gather_fusion.2 = bf16[512,512]{1,0:T(8,128)(2,1)S(1)} fusion(bf16[4096,512]{1,0:T(8,128)(2,1)} %bitcast.31, s32[1024]{0:T(1024)S(1)} %pad_clamp_fusion), kind=kCustom, calls=%fused_computation.2 | custom fusion | bytes 1050624 | tf_op jit(solution)/shard_map/gather | solution.py:425
  94.2 3.1 %gather_fusion.1 = f32[512]{0:T(512)S(1)} fusion(f32[4096]{0:T(1024)S(1)} %select_select_fusion, s32[1024]{0:T(1024)S(1)} %pad_clamp_fusion), kind=kCustom, calls=%fused_computation.1 | custom fusion | bytes 6144 | tf_op jit(solution)/shard_map/gather | solution.py:423
  97.3 4.7 %gather_fusion = bf16[512,512]{1,0:T(8,128)(2,1)S(1)} fusion(bf16[4096,512]{1,0:T(8,128)(2,1)} %bitcast.29, s32[1024]{0:T(1024)S(1)} %pad_clamp_fusion), kind=kCustom, calls=%fused_computation | custom fusion | bytes 1050624 | tf_op jit(solution)/shard_map/gather | solution.py:424
  102.1 0.2 multiply_convert_fusion
  102.3 0.8 multiply_bitcast_fusion
  103.1 0.1 copy.11.weight
  103.2 68.1 %sweeps.1 = f32[16,512]{1,0:T(8,128)S(1)} custom-call(f32[512,512]{1,0:T(8,128)S(1)} %get-tuple-element.11.dp, bf16[512,512]{1,0:T(8,128)(2,1)S(1)} %get-tuple-element.10.src_r, bf16[512,512]{1,0:T(8,128)(2,1)S(1)} %get-tuple-element.9.src_c, f32[1,512]{1,0:T(1,128)S(1)} %bitcast.27, f32[1,512]{1,0:T(1,128)S(1)} %bitcast.28, ...), custom_call_target="tpu_custom_call" | custom-call | tf_op jit(solution)/shard_map/sweeps/pallas_call | solution.py:370
  171.3 0.6 copy.26
  (4 shorter events, 0.0 us)
Async XLA Ops:
  76.4 6.1 %copy-start.1 = (f32[512,512]{1,0:T(8,128)S(1)}, f32[512,512]{1,0:T(8,128)}, u32[]{:S(2)}) copy-start(f32[512,512]{1,0:T(8,128)} %param.11) | copy-start | bytes 3145732
  82.5 7.0 %copy-start = (s32[512]{0:T(512)S(1)}, s32[512]{0:T(512)}, u32[]{:S(2)}) copy-start(s32[512]{0:T(512)} %param.9) | copy-start | bytes 6148

commit v2 on v0

v2 whole, which is shorter than its diff:
```python
import math

import jax
import jax.numpy as jnp
from jax import lax
from jax.experimental import pallas as pl
from jax.experimental.pallas import tpu as pltpu
from jax.sharding import PartitionSpec as P

NG = 8192
NRES = 512
NPAIR = 4096
MESH = pl.DeviceIdType.MESH
BF = jnp.bfloat16
F32 = jnp.float32
NSEM = 192


def bit(n, at):
    return (n // 2**at) % 2


def number(b3, b2, b1, b0):
    return (b3 % 2) * 8 + (b2 % 2) * 4 + (b1 % 2) * 2 + b0 % 2


def crossed(row, col):
    return number(
        bit(row, 3) + bit(col, 3), bit(row, 2) + bit(col, 2),
        bit(row, 0) + bit(col, 1), bit(row, 1) + bit(col, 0),
    )


class Place:
    def __init__(self):
        self.r = lax.axis_index("row")
        self.c = lax.axis_index("col")
        self.zl = self.r // 8
        self.x = (self.r // 2) % 4
        self.k = self.r % 2
        self.y = self.c // 4
        self.h = self.c % 4
        self.j = self.r // 2

    def row(self, zl=0, x=0, k=0):
        return ((self.zl + zl) % 2) * 8 + ((self.x + x) % 4) * 2 + (self.k + k) % 2

    def col(self, y=0, h=0):
        return ((self.y + y) % 4) * 4 + (self.h + h) % 4


class Links:
    def __init__(self, send, recv):
        self.send, self.recv, self.used, self.sent = send, recv, 0, []

    def new(self):
        self.used += 1
        return self.used - 1

    def copy(self, n, src, dst, to):
        return pltpu.make_async_remote_copy(
            src_ref=src, dst_ref=dst, send_sem=self.send.at[n], recv_sem=self.recv.at[n],
            device_id=to, device_id_type=MESH,
        )

    def go(self, n, src, dst, to):
        one = self.copy(n, src, dst, to)
        one.start()
        self.sent.append(one)

    def arrived(self, n, ref, to):
        self.copy(n, ref, ref, to).wait_recv()

    def drain(self):
        for one in self.sent:
            one.wait_send()
        self.sent = []


class Ring:
    def __init__(self, links, slots, step):
        self.links, self.slots, self.step = links, slots, step
        self.n = [links.new() for _ in range(4)]

    def start(self):
        for n, d in ((0, 1), (1, -1)):
            self.links.go(self.n[n], self.slots(0), self.slots(0), self.step(d))

    def half(self, d, n):
        size = self.slots(0).shape[0] // 2
        return self.slots(d).at[pl.ds(n * size, size)]

    def forward(self):
        for n, d in ((0, 1), (1, -1)):
            self.links.arrived(self.n[n], self.slots(-d), self.step(d))
            self.links.go(self.n[2 + n], self.half(-d, n), self.half(-d, n), self.step(d))

    def last(self):
        for n, d in ((0, 1), (1, -1)):
            self.links.arrived(self.n[2 + n], self.half(-2 * d, n), self.step(d))


def split(value):
    high = value.astype(BF)
    return high, (value - high.astype(F32)).astype(BF)


def nn(a, b):
    return lax.dot_general(a, b, (((1,), (0,)), ((), ())), preferred_element_type=F32)


def nt(a, b):
    return lax.dot_general(a, b, (((1,), (1,)), ((), ())), preferred_element_type=F32)


def tn(a, b):
    return lax.dot_general(a, b, (((0,), (0,)), ((), ())), preferred_element_type=F32)


def rows(start, size):
    return pl.ds(pl.multiple_of(start * size, size), size)


def iota(shape, axis):
    return lax.broadcasted_iota(jnp.int32, shape, axis)


def line(ref, start, count):
    return jnp.concatenate([ref[pl.ds(start * count + n, 1), :] for n in range(count)], axis=1)


def power(exponent, down=0.5, up=2.0):
    return jnp.where(exponent < 0, down, jnp.where(exponent > 0, up, 1.0)).astype(F32)


PEERS = [(a, b) for a in range(2) for b in range(4) if (a, b) != (0, 0)]
HALVES = range(2)


def screen_kernel(
    stop, density, exps, weights, ids, shift, background, dielectric, kernel,
    al, ar, hop, bg, dv, dh, dl, acc, src, s0, idc, pre,
    u1, xbuf, wbuf, rbuf, s1, u2, ybuf, tbuf, hbuf, both, kp, kx, ko, kbuf, kt, fin,
    send, recv, local,
):
    me = Place()
    links = Links(send, recv)
    barrier = pltpu.get_barrier_semaphore()
    for d in range(1, 16):
        pl.semaphore_signal(barrier, inc=1, device_id=((me.r + d) % 16, me.c), device_id_type=MESH)
        pl.semaphore_signal(barrier, inc=1, device_id=(me.r, (me.c + d) % 16), device_id_type=MESH)
    bg_in = pltpu.make_async_copy(background, bg, local.at[0])
    bg_in.start()
    factors = line(exps, me.c, 2)
    on_diagonal = iota((256, 256), 0) == iota((256, 256), 1)
    column = jnp.sum(jnp.where(on_diagonal, power(factors), 0.0), axis=1, keepdims=True)
    own = (density[...].astype(F32) * column).astype(BF).reshape(16, 16, 512)
    al[me.c] = own
    pl.semaphore_wait(barrier, 30)

    def part(ref, slot, p):
        return ref.at[slot, pl.ds(p * 8, 8)]

    first_to = (crossed_back(me.r, me.c), me.c)
    second_to = (me.r, crossed(me.r, me.c))
    stays = first_to[0] == me.r

    def slot_of(row):
        return crossed(row, me.c)

    mine = slot_of(me.r)

    class Panel:
        def __init__(self, p):
            self.p = p
            self.hop1, self.hop2, self.low = links.new(), links.new(), links.new()
            self.rings = [
                Ring(links, lambda d, n=n: part(ar, slot_of(me.row(zl=n, x=d)), p),
                     lambda d: (me.row(x=d), me.c))
                for n in range(2)
            ]
            self.hands = []

        def copy1(self):
            return links.copy(self.hop1, part(al, me.c, self.p), hop.at[pl.ds(self.p * 8, 8)], first_to)

        def copy2(self):
            return links.copy(self.hop2, hop.at[pl.ds(self.p * 8, 8)], part(ar, me.c, self.p), second_to)

        def hand(self, n, d):
            at = links.new()
            ref = part(ar, slot_of(me.row(zl=n, x=d)), self.p)
            links.go(at, ref, ref, (me.row(k=1), me.c))
            self.hands.append((at, part(ar, slot_of(me.row(zl=n, x=d, k=1)), self.p)))

        def step1(self):
            @pl.when(jnp.logical_not(stays))
            def _():
                self.copy1().start()

            @pl.when(stays)
            def _():
                hop[pl.ds(self.p * 8, 8)] = al[me.c, pl.ds(self.p * 8, 8)]

        def step2(self):
            here = hop.at[pl.ds(self.p * 8, 8)]

            @pl.when(jnp.logical_not(stays))
            def _():
                links.arrived(self.hop1, here, first_to)

            @pl.when(me.r != 0)
            def _():
                links.copy(self.hop2, here, part(ar, me.c, self.p), second_to).start()

            @pl.when(me.r == 0)
            def _():
                ar[mine, pl.ds(self.p * 8, 8)] = hop[pl.ds(self.p * 8, 8)]

        def step3(self):
            @pl.when(me.r != 0)
            def _():
                links.arrived(self.hop2, part(ar, mine, self.p), second_to)

            there = part(ar, mine, self.p)
            links.go(self.low, there, there, (me.row(zl=1), me.c))
            self.rings[0].start()
            self.hand(0, 0)

        def step4(self):
            links.arrived(self.low, part(ar, slot_of(me.row(zl=1)), self.p), (me.row(zl=1), me.c))
            self.rings[1].start()
            self.hand(1, 0)

        def forward(self, n):
            self.rings[n].forward()
            self.hand(n, 1)
            self.hand(n, -1)

        def last(self, n):
            self.rings[n].last()
            self.hand(n, 2)

        def end(self):
            for at, ref in self.hands:
                links.arrived(at, ref, (me.row(k=1), me.c))

        def drain(self):
            @pl.when(jnp.logical_not(stays))
            def _():
                self.copy1().wait_send()

            @pl.when(me.r != 0)
            def _():
                self.copy2().wait_send()

    panel = [Panel(p) for p in range(2)]
    zz = [
        Ring(links, lambda d, p=p: part(al, me.col(h=d), p), lambda d: (me.r, me.col(h=d)))
        for p in range(2)
    ]
    yy = [
        [
            Ring(links, lambda d, p=p, o=o: part(al, me.col(y=d, h=o), p),
                 lambda d: (me.r, me.col(y=d)))
            for o in (0, -1, 1, 2)
        ]
        for p in range(2)
    ]
    panel[0].step1()
    panel[1].step1()
    zz[0].start()
    yy[0][0].start()
    zz[1].start()
    yy[1][0].start()

    to_lane = iota((512, 512), 0)
    to_lane = (to_lane % 256) // 16 * 32 + to_lane // 256 * 16 + to_lane % 16
    wanted = jnp.where(to_lane == iota((512, 512), 1), line(ids, 0, 4), 0)
    idc[...] = jnp.broadcast_to(jnp.sum(wanted, axis=1, keepdims=True), (512, 128))
    acc[...] = jnp.zeros((512, 512), F32)
    pre[...] = jnp.zeros((2, 1, 512), F32)

    def picks(id_column, slot):
        count = id_column.shape[0]
        inverse = power(line(exps, slot, 2), 2.0, 0.5)
        hit = id_column == iota((count, 256), 1) + slot * 256
        return jnp.where(hit, inverse, 0.0).astype(BF)

    def squares(n, ref, slot):
        wide = ref[slot].reshape(256, 512).astype(F32)
        pre[n] += jnp.sum(wide * wide, axis=0, keepdims=True)

    def take(slot):
        squares(0, al, slot)
        acc[...] += nn(picks(idc[:, :1], slot), al[slot].reshape(256, 512))

    panel[0].step2()
    yy[0][0].forward()
    panel[1].step2()
    yy[1][0].forward()
    zz[0].forward()
    yy[0][1].start()
    yy[0][2].start()
    take(me.c)
    panel[0].step3()
    zz[1].forward()
    yy[1][1].start()
    yy[1][2].start()
    panel[0].step4()
    panel[1].step3()
    zz[0].last()
    yy[0][3].start()
    panel[1].step4()
    panel[0].forward(0)
    zz[1].last()
    yy[1][3].start()
    take(me.col(h=1))
    take(me.col(h=-1))
    yy[0][1].forward()
    yy[0][2].forward()
    panel[0].forward(1)
    panel[1].forward(0)
    yy[1][1].forward()
    yy[1][2].forward()
    panel[0].last(0)
    panel[1].forward(1)
    take(me.col(h=2))
    take(me.col(y=1))
    take(me.col(y=-1))
    panel[0].last(1)
    yy[0][3].forward()
    panel[1].last(0)
    panel[1].last(1)
    yy[1][3].forward()
    for o in (-1, 1, 2):
        take(me.col(y=1, h=o))
        take(me.col(y=-1, h=o))
    for n, o in enumerate((0, -1, 1, 2)):
        yy[0][n].last()
        yy[1][n].last()
        take(me.col(y=2, h=o))
    for one in panel:
        one.end()

    scale = 1.0 / (4 * NPAIR)
    shift_row = line(shift, me.r, 4)
    precond = shift_row + pre[0] * scale
    pre[0] = precond
    src[...] = acc[...].astype(BF)
    high, low = split(acc[...] / precond)
    s0[0] = high
    s0[1] = low
    bg_in.wait()
    diagonal = (iota((512, 512), 0) == iota((512, 512), 1)) & (me.r == me.c)
    response = tn(al[...].reshape(NPAIR, 512), ar[...].reshape(NPAIR, 512)) * scale
    value = bg[...] + response + jnp.where(diagonal, shift_row, 0.0)
    dv[...] = value
    high, low = split(jnp.where(diagonal, precond, 0.0) - 0.5 * value)
    dh[...] = high
    dl[...] = low
    d_out = pltpu.make_async_copy(dv, dielectric, local.at[1])
    d_out.start()

    def finish():
        links.drain()
        for one in panel:
            one.drain()
        d_out.wait()

    if stop == 0:
        kernel[...] = dv[:16, :]
        finish()
        return

    other = 1 - me.k

    def peer_j(a, b):
        return ((me.zl + a) % 2) * 4 + (me.x + b) % 4

    def swap(src_ref, dst_ref):
        at = links.new()
        links.go(at, src_ref, dst_ref, (me.row(k=1), me.c))
        return lambda: links.arrived(at, dst_ref, (me.row(k=1), me.c))

    def chain(b):
        at = pl.ds(b * 256, 256)
        u1[b] = nn(s0[0, at], dh[...]) + nn(s0[0, at], dl[...]) + nn(s0[1, at], dh[...])
        waiting = swap(u1.at[b, rows(other, 128)], xbuf.at[b])
        yield 1
        waiting()
        wbuf[b] = (u1[b, rows(me.k, 128)] + xbuf[b]).reshape(8, 16, 512)
        ns = [links.new() for _ in PEERS]
        for n, (dz, dx) in enumerate(PEERS):
            links.go(ns[n], wbuf.at[b, peer_j(dz, dx)], rbuf.at[b, n], (me.row(zl=dz, x=dx), me.c))
        if b == 0:
            for slot in range(16):
                squares(1, ar, slot)
            pre[1] = line(shift, me.c, 4) + pre[1] * scale
        q = me.k * 8 + me.j
        local_source = jnp.zeros((16, 512), F32)
        id_column = idc[rows(b * 16 + q, 16), :][:, :1]
        for slot in range(16):
            local_source += nn(picks(id_column, slot), ar[slot].reshape(256, 512))
        yield 2
        total = wbuf[b, me.j]
        for n, (dz, dx) in enumerate(PEERS):
            links.arrived(ns[n], rbuf.at[b, n], (me.row(zl=dz, x=dx), me.c))
            total = total + rbuf[b, n]
        high, low = split((0.5 * local_source + total) / pre[1])
        s1[b, q, 0] = high
        s1[b, q, 1] = low
        ns = [links.new() for _ in PEERS]
        for n, (dz, dx) in enumerate(PEERS):
            links.go(ns[n], s1.at[b, q], s1.at[b, q], (me.row(zl=dz, x=dx), me.c))
        hands = []

        def hand(j):
            n = links.new()
            links.go(n, s1.at[b, me.k * 8 + j], s1.at[b, me.k * 8 + j], (me.row(k=1), me.c))
            hands.append((n, s1.at[b, other * 8 + j]))

        hand(me.j)
        yield 3
        for n, (dz, dx) in enumerate(PEERS):
            j = peer_j(-dz, -dx)
            links.arrived(ns[n], s1.at[b, me.k * 8 + j], (me.row(zl=dz, x=dx), me.c))
            hand(j)
        yield 4
        for n, ref in hands:
            links.arrived(n, ref, (me.row(k=1), me.c))
        high = s1[b, :, 0].reshape(256, 512)
        low = s1[b, :, 1].reshape(256, 512)
        u2[b] = nt(high, dh[...]) + nt(high, dl[...]) + nt(low, dh[...])
        ns = [links.new() for _ in range(3)]
        for d in range(1, 4):
            links.go(ns[d - 1], u2.at[b, rows((me.y + d) % 4, 64)], ybuf.at[b, d - 1],
                     (me.r, me.col(y=d)))
        yield 5
        total = u2[b, rows(me.y, 64)]
        for d in range(1, 4):
            links.arrived(ns[d - 1], ybuf.at[b, d - 1], (me.r, me.col(y=d)))
            total = total + ybuf[b, d - 1]
        tbuf[b] = total.reshape(4, 16, 512)
        ns = [links.new() for _ in range(3)]
        for d in range(1, 4):
            links.go(ns[d - 1], tbuf.at[b, (me.h + d) % 4], hbuf.at[b, d - 1], (me.r, me.col(h=d)))
        yield 6
        total = tbuf[b, me.h]
        for d in range(1, 4):
            links.arrived(ns[d - 1], hbuf.at[b, d - 1], (me.r, me.col(h=d)))
            total = total + hbuf[b, d - 1]
        source = src[rows(b * 16 + me.c, 16), :].astype(F32)
        high, low = split((0.5 * source + total) / pre[0])
        both[pl.ds(b * 16, 16)] = high
        both[pl.ds(32 + b * 16, 16)] = low
        yield 7

    chains = [chain(b) for b in HALVES]
    for step in range(9):
        for b in HALVES:
            if 1 <= step - b + 1 <= 7 and step - b + 1 <= stop:
                next(chains[b])
    if stop < 8:
        kernel[...] = dv[:16, :]
        finish()
        return

    def third(ref, k):
        for j in range(8):
            product = nt(both[...], al[:, j * 2 + k].reshape(256, 512))
            ref[j] = product[:32] + product[32:]

    third(kp, other)
    waiting = swap(kp, kx)
    third(ko, me.k)
    waiting()
    ko[...] += kx[...]
    ns = [links.new() for _ in PEERS]
    for n, (dz, dx) in enumerate(PEERS):
        links.go(ns[n], ko.at[peer_j(dz, dx)], kbuf.at[n], (me.row(zl=dz, x=dx), me.c))
    total = ko[me.j]
    for n, (dz, dx) in enumerate(PEERS):
        links.arrived(ns[n], kbuf.at[n], (me.row(zl=dz, x=dx), me.c))
        total = total + kbuf[n]
    if stop == 8:
        kernel[...] = dv[:16, :]
        finish()
        return
    kt[...] = jnp.concatenate([total.T, jnp.zeros((256, 96), F32)], axis=1).reshape(16, 16, 128)
    fin[me.c] = kt[me.c]
    ns = [links.new() for _ in range(16)]
    for d in range(1, 16):
        to = (me.c + d) % 16
        links.go(ns[d], kt.at[to], fin.at[me.c], (me.r, to))
    lanes = line(weights, me.c, 2).astype(F32) * power(line(exps, me.c, 2), 2.0, 0.5)
    mask = iota((16, 256), 1) == iota((16, 256), 0) + me.r * 16
    weight = jnp.sum(jnp.where(mask, lanes, 0.0), axis=1, keepdims=True) / math.sqrt(NG)
    for d in range(1, 16):
        links.arrived(ns[d], fin.at[(me.c - d) % 16], (me.r, (me.c + d) % 16))
    kernel[...] = jnp.concatenate([fin[n][:, :32] for n in range(16)], axis=1) * weight
    finish()


def crossed_back(row, col):
    return number(
        bit(row, 3) + bit(col, 3), bit(row, 2) + bit(col, 2),
        bit(row, 0) + bit(col, 0), bit(row, 1) + bit(col, 1),
    )


def screen(density, exps, weights, ids, shift, background, stop=99):
    def body(*refs):
        screen_kernel(stop, *refs)

    dma = pltpu.SemaphoreType.DMA
    vmem = pltpu.VMEM
    inside = pl.BlockSpec(memory_space=pltpu.VMEM)
    outside = pl.BlockSpec(memory_space=pl.ANY)
    return pl.pallas_call(
        body,
        out_shape=(
            jax.ShapeDtypeStruct((512, 512), F32),
            jax.ShapeDtypeStruct((16, NRES), F32),
        ),
        in_specs=[inside] * 5 + [outside],
        out_specs=(outside, inside),
        scratch_shapes=[
            vmem((16, 16, 16, 512), BF), vmem((16, 16, 16, 512), BF), vmem((16, 16, 512), BF),
            vmem((512, 512), F32), vmem((512, 512), F32), vmem((512, 512), BF), vmem((512, 512), BF),
            vmem((512, 512), F32), vmem((512, 512), BF), vmem((2, 512, 512), BF),
            vmem((512, 128), jnp.int32), vmem((2, 1, 512), F32),
            vmem((2, 256, 512), F32), vmem((2, 128, 512), F32), vmem((2, 8, 16, 512), F32),
            vmem((2, 7, 16, 512), F32), vmem((2, 16, 2, 16, 512), BF), vmem((2, 256, 512), F32),
            vmem((2, 3, 64, 512), F32), vmem((2, 4, 16, 512), F32), vmem((2, 3, 16, 512), F32),
            vmem((64, 512), BF),
            vmem((8, 32, 256), F32), vmem((8, 32, 256), F32), vmem((8, 32, 256), F32),
            vmem((7, 32, 256), F32), vmem((16, 16, 128), F32), vmem((16, 16, 128), F32),
            dma((NSEM,)), dma((NSEM,)), dma((2,)),
        ],
        compiler_params=pltpu.CompilerParams(
            collective_id=0, has_side_effects=True, vmem_limit_bytes=56 << 20
        ),
        name="screen",
    )(density, exps, weights, ids, shift, background)


def shards(pair_density, scale_exp, pair_weight, resident_ids, diagonal_shift, background):
    return screen(
        pair_density, scale_exp.reshape(32, 128), pair_weight.reshape(32, 128),
        resident_ids.reshape(4, 128), diagonal_shift.reshape(64, 128), background,
    )


def solution(mesh):
    return jax.shard_map(
        shards,
        mesh=mesh,
        in_specs=(P("col", "row"), P(), P(), P(), P(), P("row", "col")),
        out_specs=(P("row", "col"), P(("col", "row"), None)),
        check_vma=False,
    )
```

time: 610 us -> 127 us (0.21)
  waiting for transfers between devices: 514 us -> 0 us
  Pallas kernels: 0 us -> 123 us
  blocking collectives: 27.1 us -> 0 us
  matrix products: 19.3 us -> 0 us
  between operations: 13.9 us -> 0.65 us
  local copies, waits for them, and re-layouts: 15.4 us -> 2.89 us
  starting transfers between devices: 9.27 us -> 0 us
  other arithmetic: 8.49 us -> 0 us
    psum x2 -> x0, waiting for transfers between devices: 271 us -> none  [the longest x1 172 us: shards(): lax.psum(jnp.dot(dielectric, screen_cols, precision=lax.Precision.HIGHEST...]
    all_gather x2 -> x0, waiting for transfers between devices: 177 us -> none  [the longest x1 133 us: shards(): left_all = lax.all_gather(scaled, 'col', axis=0, tiled=True)]
    pallas_call x0 -> x1, Pallas kernels: none -> 123 us  [screen(): pl.pallas_call(body, out_shape=(jax.ShapeDtypeStruct((512, 512), F32), ja...]
    unnamed x6 -> x0, waiting for transfers between devices: 66.2 us -> none
    psum x1 -> x0, blocking collectives: 27.1 us -> none  [from_root(): return lax.psum(block, axis)]
    dot_general x5 -> x0, matrix products: 19.3 us -> none  [the longest x2 7.43 us: shards(): jnp.dot(dielectric, screen_cols, precision=lax.Precision.HIGHEST)]
    all_to_all x1 -> x0, starting transfers between devices: 9.07 us -> none  [shards(): lax.all_to_all(pair_rows_all, 'col', split_axis=1, concat_axis=0, tiled=T...]
    gather x3 -> x0, local copies, waits for them, and re-layouts: 8.07 us -> none  [the longest x2 4.92 us: shards(): left_all[resident_ids].astype(jnp.float32) / factor[resident_ids][:, None]]
  transfers between devices with their start and end apart: 6 -> 0, of which waited for: 5 -> 0; matrix products, arithmetic and copies ran while one was open for 3% -> 0% of each run, Pallas kernels for 0% -> 0%
where the time goes in v2:
time: 127 us
  Pallas kernels  123 us (97%)
  local copies, waits for them, and re-layouts  2.89 us (2%)
    pallas_call x1, Pallas kernels, screen(): pl.pallas_call(body, out_shape=(jax.ShapeDtypeStruct((512, 512), F32), ja...  123 us
    unnamed x4, local copies, waits for them, and re-layouts  2.89 us

profile of v2, /device:TPU:1, one launch (start us, length us, event | category | flops | bytes accessed | tf_op | source)
XLA Modules:
  0.0 126.9 jit_solution(605175394355784633)
XLA Ops:
  0.6 123.4 %screen.1 = (f32[512,512]{1,0:T(8,128)}, f32[16,512]{1,0:T(8,128)}) custom-call(bf16[256,512]{1,0:T(8,128)(2,1)} %refs_0_.1, s32[32,128]{1,0:T(8,128)} %bitcast.5, s32[32,128]{1,0:T(8,128)} %bitcast.6, s32[4,128]{1,0:T(4,128)} %bitcast.7, f32[64,128]{1,0:T(8,128)} %bitcast.4, f32[512,512]{1,0:T(8,128)} %refs_5_.1), custom_call_target="tpu_custom_call" | custom-call | tf_op jit(solution)/shard_map/screen/pallas_call | solution.py:520
  124.0 0.0 copy-start
  124.1 2.3 %copy.10 = f32[512,512]{1,0:T(8,128)} copy(f32[512,512]{1,0:T(8,128)} %get-tuple-element.4) | data formatting | bytes 2097152
  126.3 0.0 copy-done
  126.3 0.6 copy.11
Async XLA Ops:
  124.0 2.3 %copy-start = (f32[16,512]{1,0:T(8,128)S(1)}, f32[16,512]{1,0:T(8,128)}, u32[]{:S(2)}) copy-start(f32[16,512]{1,0:T(8,128)} %get-tuple-element.5) | copy-start | bytes 98308

commit v3 on v2

--- a/solution.py
+++ b/solution.py
@@ -139,16 +139,32 @@
 
 def screen_kernel(
     stop, density, exps, weights, ids, shift, background, dielectric, kernel,
-    al, ar, hop, bg, dv, dh, dl, acc, src, s0, idc, pre,
+    al, ar, hop, bg, dv, dh, dl, acc, acc_c, src, s0, idc, pre,
     u1, xbuf, wbuf, rbuf, s1, u2, ybuf, tbuf, hbuf, both, kp, kx, ko, kbuf, kt, fin,
     send, recv, local,
 ):
     me = Place()
     links = Links(send, recv)
     barrier = pltpu.get_barrier_semaphore()
-    for d in range(1, 16):
-        pl.semaphore_signal(barrier, inc=1, device_id=((me.r + d) % 16, me.c), device_id_type=MESH)
-        pl.semaphore_signal(barrier, inc=1, device_id=(me.r, (me.c + d) % 16), device_id_type=MESH)
+    comes_from = (crossed(me.r, me.c), me.c)
+    goes_to = (crossed_back(me.r, me.c), me.c)
+    second = (me.r, crossed(me.r, me.c))
+    neighbours = [
+        (me.row(k=1), me.c), (me.row(x=1), me.c), (me.row(x=-1), me.c), (me.row(zl=1), me.c),
+        (me.r, me.col(y=1)), (me.r, me.col(y=-1)), (me.r, me.col(h=1)), (me.r, me.col(h=-1)),
+    ]
+    for to in neighbours:
+        pl.semaphore_signal(barrier, inc=1, device_id=to, device_id_type=MESH)
+
+    @pl.when(comes_from[0] != me.r)
+    def _():
+        pl.semaphore_signal(barrier, inc=1, device_id=comes_from, device_id_type=MESH)
+
+    @pl.when(second[1] != me.c)
+    def _():
+        pl.semaphore_signal(barrier, inc=1, device_id=second, device_id_type=MESH)
+
+    expected = len(neighbours) + jnp.where(goes_to[0] != me.r, 1, 0) + jnp.where(second[1] != me.c, 1, 0)
     bg_in = pltpu.make_async_copy(background, bg, local.at[0])
     bg_in.start()
     factors = line(exps, me.c, 2)
@@ -156,10 +172,16 @@
     column = jnp.sum(jnp.where(on_diagonal, power(factors), 0.0), axis=1, keepdims=True)
     own = (density[...].astype(F32) * column).astype(BF).reshape(16, 16, 512)
     al[me.c] = own
-    pl.semaphore_wait(barrier, 30)
+    pl.semaphore_wait(barrier, expected)
 
     def part(ref, slot, p):
         return ref.at[slot, pl.ds(p * 8, 8)]
+
+    def columns(p):
+        return pl.ds(p * 256, 256)
+
+    def side(ref, slot, p):
+        return ref.at[slot, :, :, columns(p)]
 
     first_to = (crossed_back(me.r, me.c), me.c)
     second_to = (me.r, crossed(me.r, me.c))
@@ -175,23 +197,23 @@
             self.p = p
             self.hop1, self.hop2, self.low = links.new(), links.new(), links.new()
             self.rings = [
-                Ring(links, lambda d, n=n: part(ar, slot_of(me.row(zl=n, x=d)), p),
+                Ring(links, lambda d, n=n: side(ar, slot_of(me.row(zl=n, x=d)), p),
                      lambda d: (me.row(x=d), me.c))
                 for n in range(2)
             ]
             self.hands = []
 
         def copy1(self):
-            return links.copy(self.hop1, part(al, me.c, self.p), hop.at[pl.ds(self.p * 8, 8)], first_to)
+            return links.copy(self.hop1, side(al, me.c, self.p), hop.at[:, :, columns(self.p)], first_to)
 
         def copy2(self):
-            return links.copy(self.hop2, hop.at[pl.ds(self.p * 8, 8)], part(ar, me.c, self.p), second_to)
+            return links.copy(self.hop2, hop.at[:, :, columns(self.p)], side(ar, me.c, self.p), second_to)
 
         def hand(self, n, d):
             at = links.new()
-            ref = part(ar, slot_of(me.row(zl=n, x=d)), self.p)
+            ref = side(ar, slot_of(me.row(zl=n, x=d)), self.p)
             links.go(at, ref, ref, (me.row(k=1), me.c))
-            self.hands.append((at, part(ar, slot_of(me.row(zl=n, x=d, k=1)), self.p)))
+            self.hands.append((at, side(ar, slot_of(me.row(zl=n, x=d, k=1)), self.p)))
 
         def step1(self):
             @pl.when(jnp.logical_not(stays))
@@ -200,10 +222,10 @@
 
             @pl.when(stays)
             def _():
-                hop[pl.ds(self.p * 8, 8)] = al[me.c, pl.ds(self.p * 8, 8)]
+                hop[:, :, columns(self.p)] = al[me.c, :, :, columns(self.p)]
 
         def step2(self):
-            here = hop.at[pl.ds(self.p * 8, 8)]
+            here = hop.at[:, :, columns(self.p)]
 
             @pl.when(jnp.logical_not(stays))
             def _():
@@ -211,24 +233,24 @@
 
             @pl.when(me.r != 0)
             def _():
-                links.copy(self.hop2, here, part(ar, me.c, self.p), second_to).start()
+                links.copy(self.hop2, here, side(ar, me.c, self.p), second_to).start()
 
             @pl.when(me.r == 0)
             def _():
-                ar[mine, pl.ds(self.p * 8, 8)] = hop[pl.ds(self.p * 8, 8)]
+                ar[mine, :, :, columns(self.p)] = hop[:, :, columns(self.p)]
 
         def step3(self):
             @pl.when(me.r != 0)
             def _():
-                links.arrived(self.hop2, part(ar, mine, self.p), second_to)
-
-            there = part(ar, mine, self.p)
+                links.arrived(self.hop2, side(ar, mine, self.p), second_to)
+
+            there = side(ar, mine, self.p)
             links.go(self.low, there, there, (me.row(zl=1), me.c))
             self.rings[0].start()
             self.hand(0, 0)
 
         def step4(self):
-            links.arrived(self.low, part(ar, slot_of(me.row(zl=1)), self.p), (me.row(zl=1), me.c))
+            links.arrived(self.low, side(ar, slot_of(me.row(zl=1)), self.p), (me.row(zl=1), me.c))
             self.rings[1].start()
             self.hand(1, 0)
 
@@ -287,13 +309,23 @@
         hit = id_column == iota((count, 256), 1) + slot * 256
         return jnp.where(hit, inverse, 0.0).astype(BF)
 
-    def squares(n, ref, slot):
-        wide = ref[slot].reshape(256, 512).astype(F32)
-        pre[n] += jnp.sum(wide * wide, axis=0, keepdims=True)
+    def squares(value):
+        wide = value.astype(F32)
+        return jnp.sum(wide * wide, axis=0, keepdims=True)
 
     def take(slot):
-        squares(0, al, slot)
+        pre[0] += squares(al[slot].reshape(256, 512))
         acc[...] += nn(picks(idc[:, :1], slot), al[slot].reshape(256, 512))
+
+    q = me.k * 8 + me.j
+    own_ids = idc[rows(q, 32), :][:, :1]
+    acc_c[...] = jnp.zeros((32, 512), F32)
+
+    def take_right(p, n, d, k):
+        slot = slot_of(me.row(zl=n, x=d, k=k))
+        value = ar[slot, :, :, columns(p)].reshape(256, 256)
+        pre[1, :, columns(p)] += squares(value)
+        acc_c[:, columns(p)] += nn(picks(own_ids, slot), value)
 
     panel[0].step2()
     yy[0][0].forward()
@@ -303,45 +335,46 @@
     yy[0][1].start()
     yy[0][2].start()
     take(me.c)
-    panel[0].step3()
     zz[1].forward()
     yy[1][1].start()
     yy[1][2].start()
-    panel[0].step4()
-    panel[1].step3()
+    panel[0].step3()
     zz[0].last()
     yy[0][3].start()
-    panel[1].step4()
-    panel[0].forward(0)
+    panel[0].step4()
+    yy[0][1].forward()
+    yy[0][2].forward()
+    panel[1].step3()
     zz[1].last()
     yy[1][3].start()
+    panel[0].forward(0)
+    panel[1].step4()
+    yy[1][1].forward()
+    yy[1][2].forward()
     take(me.col(h=1))
     take(me.col(h=-1))
-    yy[0][1].forward()
-    yy[0][2].forward()
     panel[0].forward(1)
     panel[1].forward(0)
-    yy[1][1].forward()
-    yy[1][2].forward()
+    take(me.col(h=2))
     panel[0].last(0)
+    yy[0][3].forward()
     panel[1].forward(1)
-    take(me.col(h=2))
     take(me.col(y=1))
     take(me.col(y=-1))
     panel[0].last(1)
-    yy[0][3].forward()
     panel[1].last(0)
-    panel[1].last(1)
     yy[1][3].forward()
     for o in (-1, 1, 2):
         take(me.col(y=1, h=o))
         take(me.col(y=-1, h=o))
+    for n in range(2):
+        for d in range(4):
+            take_right(0, n, d, 0)
     for n, o in enumerate((0, -1, 1, 2)):
         yy[0][n].last()
         yy[1][n].last()
         take(me.col(y=2, h=o))
-    for one in panel:
-        one.end()
+    panel[1].last(1)
 
     scale = 1.0 / (4 * NPAIR)
     shift_row = line(shift, me.r, 4)
@@ -352,15 +385,19 @@
     s0[0] = high
     s0[1] = low
     bg_in.wait()
-    diagonal = (iota((512, 512), 0) == iota((512, 512), 1)) & (me.r == me.c)
-    response = tn(al[...].reshape(NPAIR, 512), ar[...].reshape(NPAIR, 512)) * scale
-    value = bg[...] + response + jnp.where(diagonal, shift_row, 0.0)
-    dv[...] = value
-    high, low = split(jnp.where(diagonal, precond, 0.0) - 0.5 * value)
-    dh[...] = high
-    dl[...] = low
+    on_line = me.r == me.c
     d_out = pltpu.make_async_copy(dv, dielectric, local.at[1])
-    d_out.start()
+
+    def block(p):
+        diagonal = (iota((512, 256), 0) == iota((512, 256), 1) + p * 256) & on_line
+        right = ar[:, :, :, columns(p)].reshape(NPAIR, 256)
+        response = tn(al[...].reshape(NPAIR, 512), right) * scale
+        at = slice(p * 256, p * 256 + 256)
+        value = bg[:, columns(p)] + response + jnp.where(diagonal, shift_row[:, at], 0.0)
+        dv[:, columns(p)] = value
+        high, low = split(jnp.where(diagonal, precond[:, at], 0.0) - 0.5 * value)
+        dh[:, columns(p)] = high
+        dl[:, columns(p)] = low
 
     def finish():
         links.drain()
@@ -368,11 +405,6 @@
             one.drain()
         d_out.wait()
 
-    if stop == 0:
-        kernel[...] = dv[:16, :]
-        finish()
-        return
-
     other = 1 - me.k
 
     def peer_j(a, b):
@@ -383,60 +415,80 @@
         links.go(at, src_ref, dst_ref, (me.row(k=1), me.c))
         return lambda: links.arrived(at, dst_ref, (me.row(k=1), me.c))
 
-    def chain(b):
-        at = pl.ds(b * 256, 256)
-        u1[b] = nn(s0[0, at], dh[...]) + nn(s0[0, at], dl[...]) + nn(s0[1, at], dh[...])
-        waiting = swap(u1.at[b, rows(other, 128)], xbuf.at[b])
-        yield 1
+    def first(p):
+        panel[p].end()
+        block(p)
+        if p == 1:
+            d_out.start()
+        high, low = dh[:, columns(p)], dl[:, columns(p)]
+        u1[p] = nn(s0[0], high) + nn(s0[0], low) + nn(s0[1], high)
+        waiting = swap(u1.at[p, rows(other, 256)], xbuf.at[p])
+        yield
+        if p == 1:
+            for n in range(2):
+                for d in range(4):
+                    take_right(1, n, d, 0)
+        for n in range(2):
+            for d in range(4):
+                take_right(p, n, d, 1)
+        at = slice(p * 256, p * 256 + 256)
+        precond_c = line(shift, me.c, 4)[:, at] + pre[1, :, columns(p)] * scale
+        yield
         waiting()
-        wbuf[b] = (u1[b, rows(me.k, 128)] + xbuf[b]).reshape(8, 16, 512)
+        wbuf[p] = (u1[p, rows(me.k, 256)] + xbuf[p]).reshape(8, 32, 256)
         ns = [links.new() for _ in PEERS]
         for n, (dz, dx) in enumerate(PEERS):
-            links.go(ns[n], wbuf.at[b, peer_j(dz, dx)], rbuf.at[b, n], (me.row(zl=dz, x=dx), me.c))
-        if b == 0:
-            for slot in range(16):
-                squares(1, ar, slot)
-            pre[1] = line(shift, me.c, 4) + pre[1] * scale
-        q = me.k * 8 + me.j
-        local_source = jnp.zeros((16, 512), F32)
-        id_column = idc[rows(b * 16 + q, 16), :][:, :1]
-        for slot in range(16):
-            local_source += nn(picks(id_column, slot), ar[slot].reshape(256, 512))
-        yield 2
-        total = wbuf[b, me.j]
+            links.go(ns[n], wbuf.at[p, peer_j(dz, dx)], rbuf.at[p, n], (me.row(zl=dz, x=dx), me.c))
+        yield
+        total = wbuf[p, me.j]
         for n, (dz, dx) in enumerate(PEERS):
-            links.arrived(ns[n], rbuf.at[b, n], (me.row(zl=dz, x=dx), me.c))
-            total = total + rbuf[b, n]
-        high, low = split((0.5 * local_source + total) / pre[1])
-        s1[b, q, 0] = high
-        s1[b, q, 1] = low
+            links.arrived(ns[n], rbuf.at[p, n], (me.row(zl=dz, x=dx), me.c))
+            total = total + rbuf[p, n]
+        high, low = split((0.5 * acc_c[:, columns(p)] + total) / precond_c)
+        s1[p, q, 0] = high
+        s1[p, q, 1] = low
         ns = [links.new() for _ in PEERS]
         for n, (dz, dx) in enumerate(PEERS):
-            links.go(ns[n], s1.at[b, q], s1.at[b, q], (me.row(zl=dz, x=dx), me.c))
+            links.go(ns[n], s1.at[p, q], s1.at[p, q], (me.row(zl=dz, x=dx), me.c))
         hands = []
 
         def hand(j):
             n = links.new()
-            links.go(n, s1.at[b, me.k * 8 + j], s1.at[b, me.k * 8 + j], (me.row(k=1), me.c))
-            hands.append((n, s1.at[b, other * 8 + j]))
+            links.go(n, s1.at[p, me.k * 8 + j], s1.at[p, me.k * 8 + j], (me.row(k=1), me.c))
+            hands.append((n, s1.at[p, other * 8 + j]))
 
         hand(me.j)
-        yield 3
+        yield
         for n, (dz, dx) in enumerate(PEERS):
             j = peer_j(-dz, -dx)
-            links.arrived(ns[n], s1.at[b, me.k * 8 + j], (me.row(zl=dz, x=dx), me.c))
+            links.arrived(ns[n], s1.at[p, me.k * 8 + j], (me.row(zl=dz, x=dx), me.c))
             hand(j)
-        yield 4
+        yield
         for n, ref in hands:
             links.arrived(n, ref, (me.row(k=1), me.c))
-        high = s1[b, :, 0].reshape(256, 512)
-        low = s1[b, :, 1].reshape(256, 512)
-        u2[b] = nt(high, dh[...]) + nt(high, dl[...]) + nt(low, dh[...])
+        yield
+
+    def product(b, p):
+        high = s1[p, pl.ds(b * 8, 8), 0].reshape(256, 256)
+        low = s1[p, pl.ds(b * 8, 8), 1].reshape(256, 256)
+        dhp, dlp = dh[:, columns(p)], dl[:, columns(p)]
+        return nt(high, dhp) + nt(high, dlp) + nt(low, dhp)
+
+    ones = [first(p) for p in range(2)]
+    for p in (0, 0, 0, 1, 0, 1, 1, 0, 1, 0):
+        next(ones[p])
+    for b in HALVES:
+        u2[b] = product(b, 0)
+    for p in (1, 1):
+        next(ones[p])
+
+    def chain(b):
+        u2[b] += product(b, 1)
         ns = [links.new() for _ in range(3)]
         for d in range(1, 4):
             links.go(ns[d - 1], u2.at[b, rows((me.y + d) % 4, 64)], ybuf.at[b, d - 1],
                      (me.r, me.col(y=d)))
-        yield 5
+        yield
         total = u2[b, rows(me.y, 64)]
         for d in range(1, 4):
             links.arrived(ns[d - 1], ybuf.at[b, d - 1], (me.r, me.col(y=d)))
@@ -445,7 +497,7 @@
         ns = [links.new() for _ in range(3)]
         for d in range(1, 4):
             links.go(ns[d - 1], tbuf.at[b, (me.h + d) % 4], hbuf.at[b, d - 1], (me.r, me.col(h=d)))
-        yield 6
+        yield
         total = tbuf[b, me.h]
         for d in range(1, 4):
             links.arrived(ns[d - 1], hbuf.at[b, d - 1], (me.r, me.col(h=d)))
@@ -454,17 +506,11 @@
         high, low = split((0.5 * source + total) / pre[0])
         both[pl.ds(b * 16, 16)] = high
         both[pl.ds(32 + b * 16, 16)] = low
-        yield 7
+        yield
 
     chains = [chain(b) for b in HALVES]
-    for step in range(9):
-        for b in HALVES:
-            if 1 <= step - b + 1 <= 7 and step - b + 1 <= stop:
-                next(chains[b])
-    if stop < 8:
-        kernel[...] = dv[:16, :]
-        finish()
-        return
+    for b in (0, 1, 0, 1, 0, 1):
+        next(chains[b])
 
     def third(ref, k):
         for j in range(8):
@@ -483,11 +529,8 @@
     for n, (dz, dx) in enumerate(PEERS):
         links.arrived(ns[n], kbuf.at[n], (me.row(zl=dz, x=dx), me.c))
         total = total + kbuf[n]
-    if stop == 8:
-        kernel[...] = dv[:16, :]
-        finish()
-        return
-    kt[...] = jnp.concatenate([total.T, jnp.zeros((256, 96), F32)], axis=1).reshape(16, 16, 128)
+    turned = total.T.reshape(16, 4, 4, 32)
+    kt[...] = jnp.concatenate([turned[:, g] for g in range(4)], axis=-1)
     fin[me.c] = kt[me.c]
     ns = [links.new() for _ in range(16)]
     for d in range(1, 16):
@@ -498,7 +541,11 @@
     weight = jnp.sum(jnp.where(mask, lanes, 0.0), axis=1, keepdims=True) / math.sqrt(NG)
     for d in range(1, 16):
         links.arrived(ns[d], fin.at[(me.c - d) % 16], (me.r, (me.c + d) % 16))
-    kernel[...] = jnp.concatenate([fin[n][:, :32] for n in range(16)], axis=1) * weight
+    packed = [fin[n] for n in range(16)]
+    gathered = [
+        jnp.concatenate([one[:, g * 32 : g * 32 + 32] for one in packed], axis=1) for g in range(4)
+    ]
+    kernel[...] = jnp.concatenate(gathered, axis=0) * weight
     finish()
 
 
@@ -528,14 +575,14 @@
         scratch_shapes=[
             vmem((16, 16, 16, 512), BF), vmem((16, 16, 16, 512), BF), vmem((16, 16, 512), BF),
             vmem((512, 512), F32), vmem((512, 512), F32), vmem((512, 512), BF), vmem((512, 512), BF),
-            vmem((512, 512), F32), vmem((512, 512), BF), vmem((2, 512, 512), BF),
+            vmem((512, 512), F32), vmem((32, 512), F32), vmem((512, 512), BF), vmem((2, 512, 512), BF),
             vmem((512, 128), jnp.int32), vmem((2, 1, 512), F32),
-            vmem((2, 256, 512), F32), vmem((2, 128, 512), F32), vmem((2, 8, 16, 512), F32),
-            vmem((2, 7, 16, 512), F32), vmem((2, 16, 2, 16, 512), BF), vmem((2, 256, 512), F32),
+            vmem((2, 512, 256), F32), vmem((2, 256, 256), F32), vmem((2, 8, 32, 256), F32),
+            vmem((2, 7, 32, 256), F32), vmem((2, 16, 2, 32, 256), BF), vmem((2, 256, 512), F32),
             vmem((2, 3, 64, 512), F32), vmem((2, 4, 16, 512), F32), vmem((2, 3, 16, 512), F32),
             vmem((64, 512), BF),
             vmem((8, 32, 256), F32), vmem((8, 32, 256), F32), vmem((8, 32, 256), F32),
-            vmem((7, 32, 256), F32), vmem((16, 16, 128), F32), vmem((16, 16, 128), F32),
+            vmem((7, 32, 256), F32), vmem((16, 4, 128), F32), vmem((16, 4, 128), F32),
             dma((NSEM,)), dma((NSEM,)), dma((2,)),
         ],
         compiler_params=pltpu.CompilerParams(

time: 127 us -> 129 us (1.016)
  Pallas kernels: 123 us -> 125 us
    pallas_call x1, Pallas kernels: 123 us -> 125 us  [screen(): pl.pallas_call(body, out_shape=(jax.ShapeDtypeStruct((512, 512), F32), ja...]
where the time goes in v3:
time: 129 us
  Pallas kernels  125 us (97%)
  local copies, waits for them, and re-layouts  2.89 us (2%)
    pallas_call x1, Pallas kernels, screen(): pl.pallas_call(body, out_shape=(jax.ShapeDtypeStruct((512, 512), F32), ja...  125 us
    unnamed x4, local copies, waits for them, and re-layouts  2.89 us

profile of v3, /device:TPU:1, one launch (start us, length us, event | category | flops | bytes accessed | tf_op | source)
XLA Modules:
  0.0 128.9 jit_solution(11295256363876514092)
XLA Ops:
  0.6 125.4 %screen.1 = (f32[512,512]{1,0:T(8,128)}, f32[16,512]{1,0:T(8,128)}) custom-call(bf16[256,512]{1,0:T(8,128)(2,1)} %refs_0_.1, s32[32,128]{1,0:T(8,128)} %bitcast.5, s32[32,128]{1,0:T(8,128)} %bitcast.6, s32[4,128]{1,0:T(4,128)} %bitcast.7, f32[64,128]{1,0:T(8,128)} %bitcast.4, f32[512,512]{1,0:T(8,128)} %refs_5_.1), custom_call_target="tpu_custom_call" | custom-call | tf_op jit(solution)/shard_map/screen/pallas_call | solution.py:567
  126.0 0.0 copy-start
  126.1 2.3 %copy.10 = f32[512,512]{1,0:T(8,128)} copy(f32[512,512]{1,0:T(8,128)} %get-tuple-element.4) | data formatting | bytes 2097152
  128.3 0.0 copy-done
  128.3 0.6 copy.11
Async XLA Ops:
  126.0 2.3 %copy-start = (f32[16,512]{1,0:T(8,128)S(1)}, f32[16,512]{1,0:T(8,128)}, u32[]{:S(2)}) copy-start(f32[16,512]{1,0:T(8,128)} %get-tuple-element.5) | copy-start | bytes 98308

commit v4 on v2

--- a/solution.py
+++ b/solution.py
@@ -139,16 +139,32 @@
 
 def screen_kernel(
     stop, density, exps, weights, ids, shift, background, dielectric, kernel,
-    al, ar, hop, bg, dv, dh, dl, acc, src, s0, idc, pre,
+    al, ar, hop, bg, dv, dh, dl, acc, acc_c, src, s0, idc, pre,
     u1, xbuf, wbuf, rbuf, s1, u2, ybuf, tbuf, hbuf, both, kp, kx, ko, kbuf, kt, fin,
     send, recv, local,
 ):
     me = Place()
     links = Links(send, recv)
     barrier = pltpu.get_barrier_semaphore()
-    for d in range(1, 16):
-        pl.semaphore_signal(barrier, inc=1, device_id=((me.r + d) % 16, me.c), device_id_type=MESH)
-        pl.semaphore_signal(barrier, inc=1, device_id=(me.r, (me.c + d) % 16), device_id_type=MESH)
+    comes_from = (crossed(me.r, me.c), me.c)
+    goes_to = (crossed_back(me.r, me.c), me.c)
+    second = (me.r, crossed(me.r, me.c))
+    neighbours = [
+        (me.row(k=1), me.c), (me.row(x=1), me.c), (me.row(x=-1), me.c), (me.row(zl=1), me.c),
+        (me.r, me.col(y=1)), (me.r, me.col(y=-1)), (me.r, me.col(h=1)), (me.r, me.col(h=-1)),
+    ]
+    for to in neighbours:
+        pl.semaphore_signal(barrier, inc=1, device_id=to, device_id_type=MESH)
+
+    @pl.when(comes_from[0] != me.r)
+    def _():
+        pl.semaphore_signal(barrier, inc=1, device_id=comes_from, device_id_type=MESH)
+
+    @pl.when(second[1] != me.c)
+    def _():
+        pl.semaphore_signal(barrier, inc=1, device_id=second, device_id_type=MESH)
+
+    expected = len(neighbours) + jnp.where(goes_to[0] != me.r, 1, 0) + jnp.where(second[1] != me.c, 1, 0)
     bg_in = pltpu.make_async_copy(background, bg, local.at[0])
     bg_in.start()
     factors = line(exps, me.c, 2)
@@ -156,7 +172,7 @@
     column = jnp.sum(jnp.where(on_diagonal, power(factors), 0.0), axis=1, keepdims=True)
     own = (density[...].astype(F32) * column).astype(BF).reshape(16, 16, 512)
     al[me.c] = own
-    pl.semaphore_wait(barrier, 30)
+    pl.semaphore_wait(barrier, expected)
 
     def part(ref, slot, p):
         return ref.at[slot, pl.ds(p * 8, 8)]
@@ -294,6 +310,14 @@
     def take(slot):
         squares(0, al, slot)
         acc[...] += nn(picks(idc[:, :1], slot), al[slot].reshape(256, 512))
+
+    q = me.k * 8 + me.j
+    own_ids = jnp.concatenate([idc[rows(q, 16), :], idc[rows(16 + q, 16), :]], axis=0)[:, :1]
+    acc_c[...] = jnp.zeros((32, 512), F32)
+
+    def take_right(slot):
+        squares(1, ar, slot)
+        acc_c[...] += nn(picks(own_ids, slot), ar[slot].reshape(256, 512))
 
     panel[0].step2()
     yy[0][0].forward()
@@ -331,8 +355,13 @@
     panel[0].last(1)
     yy[0][3].forward()
     panel[1].last(0)
+    for n in range(2):
+        for d in (0, 1, -1):
+            take_right(slot_of(me.row(zl=n, x=d)))
     panel[1].last(1)
     yy[1][3].forward()
+    take_right(slot_of(me.row(x=2)))
+    take_right(slot_of(me.row(zl=1, x=2)))
     for o in (-1, 1, 2):
         take(me.col(y=1, h=o))
         take(me.col(y=-1, h=o))
@@ -394,20 +423,16 @@
         for n, (dz, dx) in enumerate(PEERS):
             links.go(ns[n], wbuf.at[b, peer_j(dz, dx)], rbuf.at[b, n], (me.row(zl=dz, x=dx), me.c))
         if b == 0:
-            for slot in range(16):
-                squares(1, ar, slot)
+            for n in range(2):
+                for d in range(4):
+                    take_right(slot_of(me.row(zl=n, x=d, k=1)))
             pre[1] = line(shift, me.c, 4) + pre[1] * scale
-        q = me.k * 8 + me.j
-        local_source = jnp.zeros((16, 512), F32)
-        id_column = idc[rows(b * 16 + q, 16), :][:, :1]
-        for slot in range(16):
-            local_source += nn(picks(id_column, slot), ar[slot].reshape(256, 512))
         yield 2
         total = wbuf[b, me.j]
         for n, (dz, dx) in enumerate(PEERS):
             links.arrived(ns[n], rbuf.at[b, n], (me.row(zl=dz, x=dx), me.c))
             total = total + rbuf[b, n]
-        high, low = split((0.5 * local_source + total) / pre[1])
+        high, low = split((0.5 * acc_c[pl.ds(b * 16, 16), :] + total) / pre[1])
         s1[b, q, 0] = high
         s1[b, q, 1] = low
         ns = [links.new() for _ in PEERS]
@@ -487,7 +512,8 @@
         kernel[...] = dv[:16, :]
         finish()
         return
-    kt[...] = jnp.concatenate([total.T, jnp.zeros((256, 96), F32)], axis=1).reshape(16, 16, 128)
+    turned = total.T.reshape(16, 4, 4, 32)
+    kt[...] = jnp.concatenate([turned[:, g] for g in range(4)], axis=-1)
     fin[me.c] = kt[me.c]
     ns = [links.new() for _ in range(16)]
     for d in range(1, 16):
@@ -498,7 +524,11 @@
     weight = jnp.sum(jnp.where(mask, lanes, 0.0), axis=1, keepdims=True) / math.sqrt(NG)
     for d in range(1, 16):
         links.arrived(ns[d], fin.at[(me.c - d) % 16], (me.r, (me.c + d) % 16))
-    kernel[...] = jnp.concatenate([fin[n][:, :32] for n in range(16)], axis=1) * weight
+    packed = [fin[n] for n in range(16)]
+    gathered = [
+        jnp.concatenate([one[:, g * 32 : g * 32 + 32] for one in packed], axis=1) for g in range(4)
+    ]
+    kernel[...] = jnp.concatenate(gathered, axis=0) * weight
     finish()
 
 
@@ -528,14 +558,14 @@
         scratch_shapes=[
             vmem((16, 16, 16, 512), BF), vmem((16, 16, 16, 512), BF), vmem((16, 16, 512), BF),
             vmem((512, 512), F32), vmem((512, 512), F32), vmem((512, 512), BF), vmem((512, 512), BF),
-            vmem((512, 512), F32), vmem((512, 512), BF), vmem((2, 512, 512), BF),
+            vmem((512, 512), F32), vmem((32, 512), F32), vmem((512, 512), BF), vmem((2, 512, 512), BF),
             vmem((512, 128), jnp.int32), vmem((2, 1, 512), F32),
             vmem((2, 256, 512), F32), vmem((2, 128, 512), F32), vmem((2, 8, 16, 512), F32),
             vmem((2, 7, 16, 512), F32), vmem((2, 16, 2, 16, 512), BF), vmem((2, 256, 512), F32),
             vmem((2, 3, 64, 512), F32), vmem((2, 4, 16, 512), F32), vmem((2, 3, 16, 512), F32),
             vmem((64, 512), BF),
             vmem((8, 32, 256), F32), vmem((8, 32, 256), F32), vmem((8, 32, 256), F32),
-            vmem((7, 32, 256), F32), vmem((16, 16, 128), F32), vmem((16, 16, 128), F32),
+            vmem((7, 32, 256), F32), vmem((16, 4, 128), F32), vmem((16, 4, 128), F32),
             dma((NSEM,)), dma((NSEM,)), dma((2,)),
         ],
         compiler_params=pltpu.CompilerParams(

time: 127 us -> 125 us (0.984)
  Pallas kernels: 123 us -> 121 us
    pallas_call x1, Pallas kernels: 123 us -> 121 us  [screen(): pl.pallas_call(body, out_shape=(jax.ShapeDtypeStruct((512, 512), F32), ja...]
where the time goes in v4:
time: 125 us; the launch traced here: 124 us
  Pallas kernels  121 us (97%)
  local copies, waits for them, and re-layouts  2.89 us (2%)
    pallas_call x1, Pallas kernels, screen(): pl.pallas_call(body, out_shape=(jax.ShapeDtypeStruct((512, 512), F32), ja...  121 us
    unnamed x4, local copies, waits for them, and re-layouts  2.89 us

profile of v4, /device:TPU:1, one launch (start us, length us, event | category | flops | bytes accessed | tf_op | source)
XLA Modules:
  0.0 124.5 jit_solution(16703603370884342407)
XLA Ops:
  0.6 121.0 %screen.1 = (f32[512,512]{1,0:T(8,128)}, f32[16,512]{1,0:T(8,128)}) custom-call(bf16[256,512]{1,0:T(8,128)(2,1)} %refs_0_.1, s32[32,128]{1,0:T(8,128)} %bitcast.5, s32[32,128]{1,0:T(8,128)} %bitcast.6, s32[4,128]{1,0:T(4,128)} %bitcast.7, f32[64,128]{1,0:T(8,128)} %bitcast.4, f32[512,512]{1,0:T(8,128)} %refs_5_.1), custom_call_target="tpu_custom_call" | custom-call | tf_op jit(solution)/shard_map/screen/pallas_call | solution.py:550
  121.6 0.0 copy-start
  121.6 2.3 %copy.10 = f32[512,512]{1,0:T(8,128)} copy(f32[512,512]{1,0:T(8,128)} %get-tuple-element.4) | data formatting | bytes 2097152
  123.9 0.0 copy-done
  123.9 0.6 copy.11
Async XLA Ops:
  121.6 2.3 %copy-start = (f32[16,512]{1,0:T(8,128)S(1)}, f32[16,512]{1,0:T(8,128)}, u32[]{:S(2)}) copy-start(f32[16,512]{1,0:T(8,128)} %get-tuple-element.5) | copy-start | bytes 98308

commit v5 on v4

--- a/solution.py
+++ b/solution.py
@@ -71,10 +71,11 @@
     def arrived(self, n, ref, to):
         self.copy(n, ref, ref, to).wait_recv()
 
-    def drain(self):
-        for one in self.sent:
+    def drain(self, count=None):
+        count = len(self.sent) if count is None else count
+        for one in self.sent[:count]:
             one.wait_send()
-        self.sent = []
+        self.sent = self.sent[count:]
 
 
 class Ring:
@@ -391,11 +392,14 @@
     d_out = pltpu.make_async_copy(dv, dielectric, local.at[1])
     d_out.start()
 
+    of_panels = len(links.sent)
+
     def finish():
         links.drain()
-        for one in panel:
-            one.drain()
-        d_out.wait()
+        if stop == 0:
+            for one in panel:
+                one.drain()
+            d_out.wait()
 
     if stop == 0:
         kernel[...] = dv[:16, :]
@@ -411,6 +415,8 @@
         at = links.new()
         links.go(at, src_ref, dst_ref, (me.row(k=1), me.c))
         return lambda: links.arrived(at, dst_ref, (me.row(k=1), me.c))
+
+    sums = [links.new() for _ in PEERS]
 
     def chain(b):
         at = pl.ds(b * 256, 256)
@@ -418,20 +424,24 @@
         waiting = swap(u1.at[b, rows(other, 128)], xbuf.at[b])
         yield 1
         waiting()
-        wbuf[b] = (u1[b, rows(me.k, 128)] + xbuf[b]).reshape(8, 16, 512)
-        ns = [links.new() for _ in PEERS]
-        for n, (dz, dx) in enumerate(PEERS):
-            links.go(ns[n], wbuf.at[b, peer_j(dz, dx)], rbuf.at[b, n], (me.row(zl=dz, x=dx), me.c))
-        if b == 0:
+        wbuf[:, b] = (u1[b, rows(me.k, 128)] + xbuf[b]).reshape(8, 16, 512)
+        if b == 1:
+            for n, (dz, dx) in enumerate(PEERS):
+                links.go(sums[n], wbuf.at[peer_j(dz, dx)], rbuf.at[n], (me.row(zl=dz, x=dx), me.c))
+        if b == 1:
             for n in range(2):
                 for d in range(4):
                     take_right(slot_of(me.row(zl=n, x=d, k=1)))
             pre[1] = line(shift, me.c, 4) + pre[1] * scale
+            links.drain(of_panels)
+            for one in panel:
+                one.drain()
         yield 2
-        total = wbuf[b, me.j]
+        total = wbuf[me.j, b]
         for n, (dz, dx) in enumerate(PEERS):
-            links.arrived(ns[n], rbuf.at[b, n], (me.row(zl=dz, x=dx), me.c))
-            total = total + rbuf[b, n]
+            if b == 0:
+                links.arrived(sums[n], rbuf.at[n], (me.row(zl=dz, x=dx), me.c))
+            total = total + rbuf[n, b]
         high, low = split((0.5 * acc_c[pl.ds(b * 16, 16), :] + total) / pre[1])
         s1[b, q, 0] = high
         s1[b, q, 1] = low
@@ -482,10 +492,8 @@
         yield 7
 
     chains = [chain(b) for b in HALVES]
-    for step in range(9):
-        for b in HALVES:
-            if 1 <= step - b + 1 <= 7 and step - b + 1 <= stop:
-                next(chains[b])
+    for b in (0, 1, 0, 1, 0, 1, 0, 0, 1, 1, 0, 1, 0, 1):
+        next(chains[b])
     if stop < 8:
         kernel[...] = dv[:16, :]
         finish()
@@ -515,10 +523,13 @@
     turned = total.T.reshape(16, 4, 4, 32)
     kt[...] = jnp.concatenate([turned[:, g] for g in range(4)], axis=-1)
     fin[me.c] = kt[me.c]
+    before = len(links.sent)
     ns = [links.new() for _ in range(16)]
     for d in range(1, 16):
         to = (me.c + d) % 16
         links.go(ns[d], kt.at[to], fin.at[me.c], (me.r, to))
+    links.drain(before)
+    d_out.wait()
     lanes = line(weights, me.c, 2).astype(F32) * power(line(exps, me.c, 2), 2.0, 0.5)
     mask = iota((16, 256), 1) == iota((16, 256), 0) + me.r * 16
     weight = jnp.sum(jnp.where(mask, lanes, 0.0), axis=1, keepdims=True) / math.sqrt(NG)
@@ -560,8 +571,8 @@
             vmem((512, 512), F32), vmem((512, 512), F32), vmem((512, 512), BF), vmem((512, 512), BF),
             vmem((512, 512), F32), vmem((32, 512), F32), vmem((512, 512), BF), vmem((2, 512, 512), BF),
             vmem((512, 128), jnp.int32), vmem((2, 1, 512), F32),
-            vmem((2, 256, 512), F32), vmem((2, 128, 512), F32), vmem((2, 8, 16, 512), F32),
-            vmem((2, 7, 16, 512), F32), vmem((2, 16, 2, 16, 512), BF), vmem((2, 256, 512), F32),
+            vmem((2, 256, 512), F32), vmem((2, 128, 512), F32), vmem((8, 2, 16, 512), F32),
+            vmem((7, 2, 16, 512), F32), vmem((2, 16, 2, 16, 512), BF), vmem((2, 256, 512), F32),
             vmem((2, 3, 64, 512), F32), vmem((2, 4, 16, 512), F32), vmem((2, 3, 16, 512), F32),
             vmem((64, 512), BF),
             vmem((8, 32, 256), F32), vmem((8, 32, 256), F32), vmem((8, 32, 256), F32),

time: 125 us -> 124 us (level)
  no operation moved by 1% of the time
where the time goes in v5:
time: 124 us
  Pallas kernels  121 us (98%)
  local copies, waits for them, and re-layouts  2.89 us (2%)
    pallas_call x1, Pallas kernels, screen(): pl.pallas_call(body, out_shape=(jax.ShapeDtypeStruct((512, 512), F32), ja...  121 us
    unnamed x4, local copies, waits for them, and re-layouts  2.89 us

profile of v5, /device:TPU:1, one launch (start us, length us, event | category | flops | bytes accessed | tf_op | source)
XLA Modules:
  0.0 124.2 jit_solution(4780996333605952018)
XLA Ops:
  0.6 120.7 %screen.1 = (f32[512,512]{1,0:T(8,128)}, f32[16,512]{1,0:T(8,128)}) custom-call(bf16[256,512]{1,0:T(8,128)(2,1)} %refs_0_.1, s32[32,128]{1,0:T(8,128)} %bitcast.5, s32[32,128]{1,0:T(8,128)} %bitcast.6, s32[4,128]{1,0:T(4,128)} %bitcast.7, f32[64,128]{1,0:T(8,128)} %bitcast.4, f32[512,512]{1,0:T(8,128)} %refs_5_.1), custom_call_target="tpu_custom_call" | custom-call | tf_op jit(solution)/shard_map/screen/pallas_call | solution.py:561
  121.3 0.0 copy-start
  121.4 2.3 %copy.10 = f32[512,512]{1,0:T(8,128)} copy(f32[512,512]{1,0:T(8,128)} %get-tuple-element.4) | data formatting | bytes 2097152
  123.6 0.0 copy-done
  123.6 0.6 copy.11
Async XLA Ops:
  121.3 2.3 %copy-start = (f32[16,512]{1,0:T(8,128)S(1)}, f32[16,512]{1,0:T(8,128)}, u32[]{:S(2)}) copy-start(f32[16,512]{1,0:T(8,128)} %get-tuple-element.5) | copy-start | bytes 98308
